TPU v7x, 256 devices: a whole 4x4x8 slice. The times are simulated.
256 devices in a mesh: seq: 16 (over x_hi, z), chan: 8 (over x_lo, y), dp: 2 (over core).
Axes of the slice: x: 4 (x_hi: 2, x_lo: 2; x = x_hi * 2 + x_lo), y: 4, z: 8, core: 2. Of those that a mesh axis runs over, the one named last changes fastest.
Arguments:
- query_proj: float32 [4096, 4096], P(('dp', 'seq'), 'chan'), parts along dimension 0, may hold values from -6 to 6
- key_proj: float32 [4096, 4096], P(('dp', 'seq'), 'chan'), parts along dimension 0, may hold values from -6 to 6
- value_proj: float32 [4096, 4096], P(('dp', 'seq'), 'chan'), parts along dimension 0, may hold values from -6 to 6
- filter_taps: float32 [2048, 4096], P('seq', 'chan'), may hold values from -6 to 6
- skip_gain: float32 [4096], P('chan'), may hold values from 0.25 to 2
- out_grad: float32 [4096, 4096], P(('dp', 'seq'), 'chan'), parts along dimension 0, may hold values from -6 to 6
- block_order: int32 [32], P('dp'), parts along dimension 0, may hold values from 0 to 15, each once
Outputs:
- hyena_out: bfloat16 [4096, 4096], P(('dp', 'seq'), 'chan'), parts along dimension 0
- grad_query: bfloat16 [4096, 4096], P(('dp', 'seq'), 'chan'), parts along dimension 0
- grad_key: bfloat16 [4096, 4096], P(('dp', 'seq'), 'chan'), parts along dimension 0
- grad_value: bfloat16 [4096, 4096], P(('dp', 'seq'), 'chan'), parts along dimension 0
- grad_filter: bfloat16 [4096, 4096], P(('dp', 'seq'), 'chan'), parts along dimension 0
There are 2 independent parts, one for each index of `dp`. A program takes and returns all parts, laid end to end along the dimension named above; an argument that names none is the same for every part. Nothing has to cross between parts.
Inputs may be any that keep to these rules, and one draw needn't show every extreme that they name: `block_order`: each loop position holds a different sequence block; every block index appears once.
All inputs are finite; a program needn't handle non-finite values.
Results may differ from a plain program's by a relative error of at most 0.0075.
Values may be sent and summed in bfloat16 or wider, within the bound.
A program may use at most 64 MiB of HBM per device.

v0:
```python
import math

import jax
import jax.numpy as jnp
from jax import lax
from jax.sharding import PartitionSpec as P


def from_behind(array, axis, by):
    peers = lax.axis_size(axis)
    return lax.ppermute(array, axis, [(i, (i + by) % peers) for i in range(peers)])


def transform_table(spectrum_length, input_length):
    frequency = lax.broadcasted_iota(jnp.float32, (spectrum_length, input_length), 0)
    time_index = lax.broadcasted_iota(jnp.float32, (spectrum_length, input_length), 1)
    angles = 2.0 * math.pi / spectrum_length * jnp.mod(frequency * time_index, spectrum_length)
    return jnp.concatenate([jnp.cos(angles), -jnp.sin(angles)], axis=0).astype(jnp.bfloat16)


def inverse_table(points, spectrum_length):
    frequency = lax.broadcasted_iota(jnp.float32, (points.shape[0], spectrum_length), 1)
    angles = 2.0 * math.pi / spectrum_length * jnp.mod(points[:, None] * frequency, spectrum_length)
    table_values = jnp.concatenate([jnp.cos(angles), -jnp.sin(angles)], axis=1) / spectrum_length
    return table_values.astype(jnp.bfloat16)


def complex_mul(first_spec, second_spec):
    half_len = first_spec.shape[-2] // 2
    first_re = first_spec[..., :half_len, :]
    first_im = first_spec[..., half_len:, :]
    second_re = second_spec[..., :half_len, :]
    second_im = second_spec[..., half_len:, :]
    return jnp.concatenate(
        [first_re * second_re - first_im * second_im, first_re * second_im + first_im * second_re],
        axis=-2,
    )


def conjugate(spectrum):
    half_len = spectrum.shape[-2] // 2
    return jnp.concatenate([spectrum[..., :half_len, :], -spectrum[..., half_len:, :]], axis=-2)


def alternating(spectrum_length):
    frequency = lax.broadcasted_iota(jnp.float32, (spectrum_length, 1), 0)
    sign_half = 1.0 - 2.0 * jnp.mod(frequency, 2.0)
    return jnp.concatenate([sign_half, sign_half], axis=0)


def advance(pieces):
    return from_behind(pieces, "seq", 1)


def on_device(query_proj, key_proj, value_proj, filter_taps, skip_gain, out_grad, block_order):
    block_rows, channels = query_proj.shape
    loop_size = lax.axis_size("seq")
    spectrum_length = 2 * block_rows
    tap_scale = 1.0 / math.sqrt(block_rows * loop_size)
    mixed = (key_proj * value_proj).astype(jnp.bfloat16)
    gated = (out_grad * query_proj).astype(jnp.bfloat16)
    scaled_taps = (filter_taps * tap_scale).astype(jnp.bfloat16)
    half_table = transform_table(spectrum_length, block_rows)
    full_table = transform_table(spectrum_length, spectrum_length)
    row_points = lax.broadcasted_iota(jnp.float32, (block_rows,), 0)
    output_table = inverse_table(row_points + block_rows, spectrum_length)
    gradient_table = inverse_table(block_rows - row_points, spectrum_length)
    taps_table = inverse_table(
        lax.broadcasted_iota(jnp.float32, (spectrum_length,), 0), spectrum_length
    )
    sign_column = alternating(spectrum_length)
    own_index = lax.axis_index("seq")
    every_tap = lax.all_gather(scaled_taps, "seq", axis=0, tiled=True)
    padded_taps = jnp.concatenate(
        [jnp.zeros((block_rows, channels), jnp.bfloat16), every_tap], axis=0
    )
    own_order = block_order[own_index]
    own_gated = sign_column * jnp.dot(half_table, gated, preferred_element_type=jnp.float32)

    def window(lag_index):
        window_rows = lax.dynamic_slice_in_dim(
            padded_taps, lag_index * block_rows, spectrum_length, 0
        )
        return jnp.dot(full_table, window_rows, preferred_element_type=jnp.float32)

    def visit(carried, pieces, source):
        out_spec, grad_spec, partial_value = carried
        lag_index = own_order - block_order[source]
        ahead_mask = (lag_index >= 0).astype(jnp.float32)
        behind_mask = (lag_index <= 0).astype(jnp.float32)
        ahead_lag = jnp.clip(lag_index, 0, loop_size - 1)
        behind_lag = jnp.clip(-lag_index, 0, loop_size - 1)
        mixed_spec = jnp.dot(half_table, pieces[0], preferred_element_type=jnp.float32)
        gated_spec = jnp.dot(half_table, pieces[1], preferred_element_type=jnp.float32)
        out_spec = out_spec + ahead_mask * complex_mul(mixed_spec, window(ahead_lag))
        grad_spec = grad_spec + behind_mask * complex_mul(conjugate(gated_spec), window(behind_lag))
        product = complex_mul(conjugate(mixed_spec), own_gated).astype(jnp.bfloat16)
        lag_taps = jnp.dot(taps_table, product, preferred_element_type=jnp.float32) * ahead_mask
        offset = ahead_lag * block_rows
        current = lax.dynamic_slice_in_dim(partial_value, offset, spectrum_length, 0)
        partial_value = lax.dynamic_update_slice_in_dim(
            partial_value, current + lag_taps, offset, 0
        )
        return (out_spec, grad_spec, partial_value)

    zero_spec = jnp.zeros((2 * spectrum_length, channels), jnp.float32)
    start_state = (
        zero_spec,
        zero_spec,
        jnp.zeros(((loop_size + 1) * block_rows, channels), jnp.float32),
    )
    both_blocks = jnp.stack([mixed, gated], axis=0)
    carried = visit(start_state, both_blocks, own_index)

    def step_one(stride, loop_carry):
        inner, upward = loop_carry
        upward = advance(upward)
        return (visit(inner, upward, jnp.mod(own_index - stride, loop_size)), upward)

    carried, upward = lax.fori_loop(1, loop_size, step_one, (carried, both_blocks))
    out_spec, grad_spec, partial_value = carried
    gain_row = skip_gain[None, :]
    conv_out = jnp.dot(
        output_table, out_spec.astype(jnp.bfloat16), preferred_element_type=jnp.float32
    ) + gain_row * mixed.astype(jnp.float32)
    conv_grad = jnp.dot(
        gradient_table, grad_spec.astype(jnp.bfloat16), preferred_element_type=jnp.float32
    ) + gain_row * gated.astype(jnp.float32)
    filter_sum = lax.psum_scatter(
        partial_value[block_rows:], "seq", scatter_dimension=0, tiled=True
    )
    grad_filter = (filter_sum * tap_scale).astype(jnp.bfloat16)
    hyena_out = (query_proj * conv_out).astype(jnp.bfloat16)
    grad_query = (out_grad * conv_out).astype(jnp.bfloat16)
    grad_key = (conv_grad * value_proj).astype(jnp.bfloat16)
    grad_value = (conv_grad * key_proj).astype(jnp.bfloat16)
    return (hyena_out, grad_query, grad_key, grad_value, grad_filter)


def solution(mesh):
    placed = (
        P(("dp", "seq"), "chan"),
        P(("dp", "seq"), "chan"),
        P(("dp", "seq"), "chan"),
        P("seq", "chan"),
        P("chan"),
        P(("dp", "seq"), "chan"),
        P("dp"),
    )
    return jax.shard_map(
        on_device,
        mesh=mesh,
        in_specs=placed,
        out_specs=(
            P(("dp", "seq"), "chan"),
            P(("dp", "seq"), "chan"),
            P(("dp", "seq"), "chan"),
            P(("dp", "seq"), "chan"),
            P(("dp", "seq"), "chan"),
        ),
        check_vma=False,
    )
```

profile of v0, /device:TPU:8, one launch (start us, length us, event | category | flops | bytes accessed | tf_op | source)
XLA Modules:
  0.0 650.5 jit_solution(4866355923954364021)
XLA Ops:
  7.2 1.6 multiply_convert_fusion.6
  18.4 81.2 %all-gather.2.cloned.1.call-done = bf16[2048,512]{1,0:T(8,128)(2,1)} async-done(((bf16[128,512]{1,0:T(8,128)(2,1)}), bf16[2048,512]{1,0:T(8,128)(2,1)}) %all-gather.2.cloned.1.call-update) | async-done | bytes 2097168 | tf_op jit(solution)/shard_map/all_gather | solution.py:73
  99.6 1.3 fusion.24
  101.1 1.6 subtract_convert_fusion.1
  104.0 2.6 dynamic_update_slice.13.clone2
  108.7 1.5 concatenate.67
  110.2 323.9 %while.21 = (s32[]{:T(128)}, f32[512,512]{1,0:T(8,128)}, f32[512,512]{1,0:T(8,128)}, f32[2176,512]{1,0:T(8,128)}, bf16[2,128,512]{2,1,0:T(8,128)(2,1)}, /*index=...) while((s32[]{:T(128)}, f32[512,512]{1,0:T(8,128)}, ...), condition=%wide.region_1.2_spmd, body=%wide.region_0.1_spmd.sunk | while | flops 542638080 | bytes 40108764 | solution.py:120
  116.8 3.6 collective-permute-done
  121.1 2.5 subtract_convert_fusion.3
  123.6 1.3 fusion.92
  127.4 3.4 fusion.91
  137.3 4.5 collective-permute-done
  142.5 2.5 subtract_convert_fusion.3
  145.0 1.3 fusion.92
  148.8 3.4 fusion.91
  158.7 4.5 collective-permute-done
  163.9 2.5 subtract_convert_fusion.3
  166.4 1.3 fusion.92
  170.2 3.4 fusion.91
  180.1 4.5 collective-permute-done
  185.3 2.5 subtract_convert_fusion.3
  191.6 3.4 fusion.91
  201.5 4.5 collective-permute-done
  206.7 2.5 subtract_convert_fusion.3
  213.0 3.4 fusion.91
  222.8 4.5 collective-permute-done
  228.0 2.5 subtract_convert_fusion.3
  234.4 3.4 fusion.91
  244.2 4.5 collective-permute-done
  249.4 2.5 subtract_convert_fusion.3
  251.9 1.3 fusion.92
  255.7 3.4 fusion.91
  265.6 4.5 collective-permute-done
  270.8 2.5 subtract_convert_fusion.3
  277.1 3.4 fusion.91
  287.0 4.5 collective-permute-done
  292.2 2.5 subtract_convert_fusion.3
  294.7 1.3 fusion.92
  298.5 3.4 fusion.91
  308.4 4.5 collective-permute-done
  313.6 2.5 subtract_convert_fusion.3
  319.9 3.4 fusion.91
  329.7 4.5 collective-permute-done
  334.9 2.5 subtract_convert_fusion.3
  341.3 3.4 fusion.91
  351.1 4.5 collective-permute-done
  356.3 2.5 subtract_convert_fusion.3
  362.6 3.4 fusion.91
  372.5 5.5 collective-permute-done
  378.7 2.5 subtract_convert_fusion.3
  385.0 3.4 fusion.91
  394.9 6.7 %collective-permute-done = bf16[2,128,512]{2,1,0:T(8,128)(2,1)S(1)} collective-permute-done((bf16[2,128,512]{2,1,0:T(8,128)(2,1)}, bf16[2,128,512]{2,1,0:T(8,128)(2,1)S(1)}, u32[]{:S(2)}, u32[]{:S(2)}) %collective-permute-start) | collective-permute-done | bytes 262176 | tf_op jit(solution)/shard_map/while/body/eval_jaxpr/ppermute | solution.py:11
  402.3 2.5 subtract_convert_fusion.3
  404.8 1.3 fusion.92
  408.6 3.4 fusion.91
  418.5 4.5 collective-permute-done
  423.7 2.5 subtract_convert_fusion.3
  426.2 1.3 fusion.92
  430.0 3.4 fusion.91
  434.2 4.7 slice.162
  440.2 2.2 multiply_convert_fusion.1
  442.4 2.2 multiply_convert_fusion.3
  444.5 197.5 %reduce-scatter.2.cloned.1.call-done = f32[128,512]{1,0:T(8,128)} async-done(((f32[2048,512]{1,0:T(8,128)}), f32[128,512]{1,0:T(8,128)}) %reduce-scatter.2.cloned.1.call-update) | async-done | bytes 262160 | tf_op jit(solution)/shard_map/reduce_scatter | solution.py:129
  642.0 1.6 multiply_convert_fusion
  (390 shorter events, 151.1 us)
Async XLA Ops:
  7.2 92.4 %all-gather.2.cloned.1.call-start = ((), (), s32[]{:S(2)}) async-start(), calls=%async_computation.1 | async-start | bytes 2228224 | tf_op jit(solution)/shard_map/all_gather | solution.py:73
  8.9 633.2 %reduce-scatter.2.cloned.1.call-start = ((), (), s32[]{:S(2)}) async-start(), calls=%async_computation.2 | async-start | bytes 4456448 | tf_op jit(solution)/shard_map/reduce_scatter | solution.py:129
  12.0 6.2 copy-start.10
  12.0 6.2 copy-start.11
  14.9 3.5 copy-start.8
  104.0 4.7 copy-start.5
  106.6 3.6 copy-start.17
  110.2 4.0 copy-start.1
  110.2 10.2 %collective-permute-start = (bf16[2,128,512]{2,1,0:T(8,128)(2,1)}, bf16[2,128,512]{2,1,0:T(8,128)(2,1)S(1)}, u32[]{:S(2)}, u32[]{:S(2)}) collective-permute-start(bf16[2,128,512]{2,1,0:T(8,128)(2,1)} %get-tuple-element.523), channel_id=1, source_target_pairs={{0,16},{16,32},{32,48},{48,64},{64,80},{80,96},{96,112},{112,128},... | collective-permute-start | bytes 786440 | tf_op jit(solution)/shard_map/while/body/eval_jaxpr/ppermute | solution.py:11
  127.1 3.7 copy-start.4
  127.4 4.2 copy-start.2
  131.6 3.1 copy-start.1
  131.6 10.2 %collective-permute-start = (bf16[2,128,512]{2,1,0:T(8,128)(2,1)}, bf16[2,128,512]{2,1,0:T(8,128)(2,1)S(1)}, u32[]{:S(2)}, u32[]{:S(2)}) collective-permute-start(bf16[2,128,512]{2,1,0:T(8,128)(2,1)} %get-tuple-element.523), channel_id=1, source_target_pairs={{0,16},{16,32},{32,48},{48,64},{64,80},{80,96},{96,112},{112,128},... | collective-permute-start | bytes 786440 | tf_op jit(solution)/shard_map/while/body/eval_jaxpr/ppermute | solution.py:11
  148.5 3.7 copy-start.4
  148.8 4.2 copy-start.2
  153.0 3.1 copy-start.1
  153.0 10.2 %collective-permute-start = (bf16[2,128,512]{2,1,0:T(8,128)(2,1)}, bf16[2,128,512]{2,1,0:T(8,128)(2,1)S(1)}, u32[]{:S(2)}, u32[]{:S(2)}) collective-permute-start(bf16[2,128,512]{2,1,0:T(8,128)(2,1)} %get-tuple-element.523), channel_id=1, source_target_pairs={{0,16},{16,32},{32,48},{48,64},{64,80},{80,96},{96,112},{112,128},... | collective-permute-start | bytes 786440 | tf_op jit(solution)/shard_map/while/body/eval_jaxpr/ppermute | solution.py:11
  169.9 3.7 copy-start.4
  170.2 4.2 copy-start.2
  174.4 3.1 copy-start.1
  174.4 10.2 %collective-permute-start = (bf16[2,128,512]{2,1,0:T(8,128)(2,1)}, bf16[2,128,512]{2,1,0:T(8,128)(2,1)S(1)}, u32[]{:S(2)}, u32[]{:S(2)}) collective-permute-start(bf16[2,128,512]{2,1,0:T(8,128)(2,1)} %get-tuple-element.523), channel_id=1, source_target_pairs={{0,16},{16,32},{32,48},{48,64},{64,80},{80,96},{96,112},{112,128},... | collective-permute-start | bytes 786440 | tf_op jit(solution)/shard_map/while/body/eval_jaxpr/ppermute | solution.py:11
  191.3 3.7 copy-start.4
  191.6 4.2 copy-start.2
  195.7 3.1 copy-start.1
  195.8 10.2 %collective-permute-start = (bf16[2,128,512]{2,1,0:T(8,128)(2,1)}, bf16[2,128,512]{2,1,0:T(8,128)(2,1)S(1)}, u32[]{:S(2)}, u32[]{:S(2)}) collective-permute-start(bf16[2,128,512]{2,1,0:T(8,128)(2,1)} %get-tuple-element.523), channel_id=1, source_target_pairs={{0,16},{16,32},{32,48},{48,64},{64,80},{80,96},{96,112},{112,128},... | collective-permute-start | bytes 786440 | tf_op jit(solution)/shard_map/while/body/eval_jaxpr/ppermute | solution.py:11
  212.7 3.7 copy-start.4
  213.0 4.2 copy-start.2
  217.1 10.2 %collective-permute-start = (bf16[2,128,512]{2,1,0:T(8,128)(2,1)}, bf16[2,128,512]{2,1,0:T(8,128)(2,1)S(1)}, u32[]{:S(2)}, u32[]{:S(2)}) collective-permute-start(bf16[2,128,512]{2,1,0:T(8,128)(2,1)} %get-tuple-element.523), channel_id=1, source_target_pairs={{0,16},{16,32},{32,48},{48,64},{64,80},{80,96},{96,112},{112,128},... | collective-permute-start | bytes 786440 | tf_op jit(solution)/shard_map/while/body/eval_jaxpr/ppermute | solution.py:11
  234.0 3.7 copy-start.4
  234.3 4.2 copy-start.2
  238.5 3.1 copy-start.1
  238.5 10.2 %collective-permute-start = (bf16[2,128,512]{2,1,0:T(8,128)(2,1)}, bf16[2,128,512]{2,1,0:T(8,128)(2,1)S(1)}, u32[]{:S(2)}, u32[]{:S(2)}) collective-permute-start(bf16[2,128,512]{2,1,0:T(8,128)(2,1)} %get-tuple-element.523), channel_id=1, source_target_pairs={{0,16},{16,32},{32,48},{48,64},{64,80},{80,96},{96,112},{112,128},... | collective-permute-start | bytes 786440 | tf_op jit(solution)/shard_map/while/body/eval_jaxpr/ppermute | solution.py:11
  255.4 3.7 copy-start.4
  255.7 4.2 copy-start.2
  259.9 10.2 %collective-permute-start = (bf16[2,128,512]{2,1,0:T(8,128)(2,1)}, bf16[2,128,512]{2,1,0:T(8,128)(2,1)S(1)}, u32[]{:S(2)}, u32[]{:S(2)}) collective-permute-start(bf16[2,128,512]{2,1,0:T(8,128)(2,1)} %get-tuple-element.523), channel_id=1, source_target_pairs={{0,16},{16,32},{32,48},{48,64},{64,80},{80,96},{96,112},{112,128},... | collective-permute-start | bytes 786440 | tf_op jit(solution)/shard_map/while/body/eval_jaxpr/ppermute | solution.py:11
  276.8 3.7 copy-start.4
  277.1 4.2 copy-start.2
  281.3 3.1 copy-start.1
  281.3 10.2 %collective-permute-start = (bf16[2,128,512]{2,1,0:T(8,128)(2,1)}, bf16[2,128,512]{2,1,0:T(8,128)(2,1)S(1)}, u32[]{:S(2)}, u32[]{:S(2)}) collective-permute-start(bf16[2,128,512]{2,1,0:T(8,128)(2,1)} %get-tuple-element.523), channel_id=1, source_target_pairs={{0,16},{16,32},{32,48},{48,64},{64,80},{80,96},{96,112},{112,128},... | collective-permute-start | bytes 786440 | tf_op jit(solution)/shard_map/while/body/eval_jaxpr/ppermute | solution.py:11
  298.2 3.7 copy-start.4
  298.5 4.2 copy-start.2
  302.7 10.2 %collective-permute-start = (bf16[2,128,512]{2,1,0:T(8,128)(2,1)}, bf16[2,128,512]{2,1,0:T(8,128)(2,1)S(1)}, u32[]{:S(2)}, u32[]{:S(2)}) collective-permute-start(bf16[2,128,512]{2,1,0:T(8,128)(2,1)} %get-tuple-element.523), channel_id=1, source_target_pairs={{0,16},{16,32},{32,48},{48,64},{64,80},{80,96},{96,112},{112,128},... | collective-permute-start | bytes 786440 | tf_op jit(solution)/shard_map/while/body/eval_jaxpr/ppermute | solution.py:11
  319.6 3.7 copy-start.4
  319.9 4.2 copy-start.2
  324.0 3.1 copy-start.1
  324.0 10.2 %collective-permute-start = (bf16[2,128,512]{2,1,0:T(8,128)(2,1)}, bf16[2,128,512]{2,1,0:T(8,128)(2,1)S(1)}, u32[]{:S(2)}, u32[]{:S(2)}) collective-permute-start(bf16[2,128,512]{2,1,0:T(8,128)(2,1)} %get-tuple-element.523), channel_id=1, source_target_pairs={{0,16},{16,32},{32,48},{48,64},{64,80},{80,96},{96,112},{112,128},... | collective-permute-start | bytes 786440 | tf_op jit(solution)/shard_map/while/body/eval_jaxpr/ppermute | solution.py:11
  341.0 3.7 copy-start.4
  341.2 4.2 copy-start.2
  345.4 10.2 %collective-permute-start = (bf16[2,128,512]{2,1,0:T(8,128)(2,1)}, bf16[2,128,512]{2,1,0:T(8,128)(2,1)S(1)}, u32[]{:S(2)}, u32[]{:S(2)}) collective-permute-start(bf16[2,128,512]{2,1,0:T(8,128)(2,1)} %get-tuple-element.523), channel_id=1, source_target_pairs={{0,16},{16,32},{32,48},{48,64},{64,80},{80,96},{96,112},{112,128},... | collective-permute-start | bytes 786440 | tf_op jit(solution)/shard_map/while/body/eval_jaxpr/ppermute | solution.py:11
  362.3 3.7 copy-start.4
  362.6 4.2 copy-start.2
  366.8 3.1 copy-start.1
  366.8 11.2 %collective-permute-start = (bf16[2,128,512]{2,1,0:T(8,128)(2,1)}, bf16[2,128,512]{2,1,0:T(8,128)(2,1)S(1)}, u32[]{:S(2)}, u32[]{:S(2)}) collective-permute-start(bf16[2,128,512]{2,1,0:T(8,128)(2,1)} %get-tuple-element.523), channel_id=1, source_target_pairs={{0,16},{16,32},{32,48},{48,64},{64,80},{80,96},{96,112},{112,128},... | collective-permute-start | bytes 786440 | tf_op jit(solution)/shard_map/while/body/eval_jaxpr/ppermute | solution.py:11
  384.7 3.7 copy-start.4
  385.0 4.2 copy-start.2
  389.2 12.4 %collective-permute-start = (bf16[2,128,512]{2,1,0:T(8,128)(2,1)}, bf16[2,128,512]{2,1,0:T(8,128)(2,1)S(1)}, u32[]{:S(2)}, u32[]{:S(2)}) collective-permute-start(bf16[2,128,512]{2,1,0:T(8,128)(2,1)} %get-tuple-element.523), channel_id=1, source_target_pairs={{0,16},{16,32},{32,48},{48,64},{64,80},{80,96},{96,112},{112,128},... | collective-permute-start | bytes 786440 | tf_op jit(solution)/shard_map/while/body/eval_jaxpr/ppermute | solution.py:11
  408.3 3.7 copy-start.4
  408.6 4.2 copy-start.2
  412.8 10.2 %collective-permute-start = (bf16[2,128,512]{2,1,0:T(8,128)(2,1)}, bf16[2,128,512]{2,1,0:T(8,128)(2,1)S(1)}, u32[]{:S(2)}, u32[]{:S(2)}) collective-permute-start(bf16[2,128,512]{2,1,0:T(8,128)(2,1)} %get-tuple-element.523), channel_id=1, source_target_pairs={{0,16},{16,32},{32,48},{48,64},{64,80},{80,96},{96,112},{112,128},... | collective-permute-start | bytes 786440 | tf_op jit(solution)/shard_map/while/body/eval_jaxpr/ppermute | solution.py:11
  429.7 3.7 copy-start.4
  430.0 4.2 copy-start.2
  438.8 3.5 copy-start.7
  438.8 3.5 copy-start.14
  438.8 3.5 copy-start.15
  (41 other events, 74.7 us)
Sparse Core Ops, SparseCore 0:
  11.2 88.3 all-gather.1
  439.0 202.9 reduce-scatter.1
where the time goes:
time: 654 us; the launch traced here: 650 us
  waiting for transfers between devices  348 us (53%)
  other arithmetic  108 us (17%)
  matrix products  87 us (13%)
  local copies, waits for them, and re-layouts  72.3 us (11%)
  loops' own time  19.9 us (3%)
  between operations  14.2 us (2%)
    reduce_scatter x1, waiting for transfers between devices, on_device(): lax.psum_scatter(partial_value[block_rows:], 'seq', scatter_dimension=0,...  197 us
    all_gather x1, waiting for transfers between devices, on_device(): every_tap = lax.all_gather(scaled_taps, 'seq', axis=0, tiled=True)  81.2 us
    ppermute x15, waiting for transfers between devices, from_behind(): lax.ppermute(array, axis, [(i, (i + by) % peers) for i in range(peers)])  69.7 us
    add x15, other arithmetic, visit(): out_spec + ahead_mask * complex_mul(mixed_spec, window(ahead_lag))  51.5 us
    another operation x18, other arithmetic  40.5 us
    dot_general x31, matrix products, window(): return jnp.dot(full_table, window_rows, preferred_element_type=jnp.float32)  38.6 us
    dot_general x16, matrix products, visit(): jnp.dot(taps_table, product, preferred_element_type=jnp.float32)  20.7 us
    another operation x1, loops' own time, on_device(): lax.fori_loop(1, loop_size, step_one, (carried, both_blocks))  19.9 us
  transfers between devices with their start and end apart: 17, of which 17 were waited for; matrix products, arithmetic and copies ran while one was open for 13% of the time, Pallas kernels for 0%

commit v1 on v0

v1 whole, which is shorter than its diff:
```python
import functools
import math

import jax
import jax.numpy as jnp
import ml_dtypes
import numpy as np
from jax import lax
from jax.experimental import pallas as pl
from jax.experimental.pallas import tpu as pltpu
from jax.sharding import PartitionSpec as P

MESH = pl.DeviceIdType.MESH
HALVES = 2


def spectrum_tables(rows):
    length = 2 * rows
    time = np.arange(rows)[:, None]
    freq = np.arange(rows)[None, :]
    angle = 2.0 * np.pi / length * ((time * freq) % length)
    middle = 1.0 - 2.0 * (time % 2)
    sine = np.where(freq == 0, middle, -np.sin(angle))
    forward = np.concatenate([np.cos(angle), sine], axis=1)
    sign = 1.0 - 2.0 * (freq % 2)
    weight = np.where(freq == 0, 1.0, 2.0) / length
    output = np.concatenate([weight * sign * np.cos(angle), weight * sign * sine], axis=1).T
    lag_sine = np.where(freq == 0, middle, np.sin(angle))
    lags = np.concatenate([weight * np.cos(angle), weight * lag_sine], axis=1).T
    return [t.astype(ml_dtypes.bfloat16) for t in (forward, output, lags)]


def kernel(
    n, q_ref, k_ref, v_ref, o_ref, taps_ref, gain_ref, order_ref, fwd_ref, out_tab_ref, lag_tab_ref,
    hyena_ref, gq_ref, gk_ref, gv_ref, gf_ref,
    send_in, recv_a, recv_b, send_out, back, mixed_s, gated_s, resp_s, sum_s, sum_g, sum_f,
    send_sem, recv_sem, back_send, back_recv,
):
    me = lax.axis_index("seq")
    rows, channels = q_ref.shape
    own = channels // n
    part = own // HALVES
    scale = 1.0 / math.sqrt(rows * n)
    bf16, f32 = jnp.bfloat16, jnp.float32

    barrier = pltpu.get_barrier_semaphore()
    for step in range(1, n):
        pl.semaphore_signal(barrier, inc=1, device_id={"seq": lax.rem(me + step, n)}, device_id_type=MESH)

    for a in range(3):
        for g in range(channels // 128):
            cols = slice(g * 128, (g + 1) * 128)
            if a == 0:
                block = k_ref[:, cols] * v_ref[:, cols]
            elif a == 1:
                block = o_ref[:, cols] * q_ref[:, cols]
            else:
                block = taps_ref[:, cols] * scale
            turned = block.T.astype(bf16)
            for i in range(128 // part):
                peer, half = (g * 128 + i * part) // own, i % HALVES
                send_in[half, peer, a * part:(a + 1) * part, :] = turned[i * part:(i + 1) * part]

    pl.semaphore_wait(barrier, n - 1)

    recvs = (recv_a, recv_b)
    hops = [(h, z) for z in (4, 3, 5, 2, 6, 1, 7, 0) for h in (1, 0) if (h, z) != (0, 0)]

    def peer_of(hop):
        h, z = hop
        ring = n // 2
        return lax.rem(me // ring + h, 2) * ring + lax.rem(me + z, ring)

    for half in range(HALVES):
        for hop in hops:
            peer = peer_of(hop)
            pltpu.make_async_remote_copy(
                src_ref=send_in.at[half, peer], dst_ref=recvs[half].at[me],
                send_sem=send_sem, recv_sem=recv_sem.at[half],
                device_id={"seq": peer}, device_id_type=MESH,
            ).start()
    for half in range(HALVES):
        recvs[half][me] = send_in[half, me]

    order = [order_ref[p] for p in range(n)]
    holder = []
    for j in range(n):
        at = jnp.int32(0)
        for p in range(1, n):
            at = jnp.where(order[p] == j, p, at)
        holder.append(at)

    lane = lax.broadcasted_iota(jnp.int32, (8, 128), 1)
    first = lane == 0
    sign = jnp.where(lane % 2 == 0, 1.0, -1.0).astype(f32)
    wide_lane = lax.broadcasted_iota(jnp.int32, (n * part, 2 * rows), 1)
    wide_sign = jnp.where(wide_lane % 2 == 0, 1.0, -1.0).astype(f32)
    re, im = slice(0, 128), slice(128, 256)

    for half in range(HALVES):
        recv = recvs[half]
        landed = recv.at[pl.ds(0, n - 1)]
        pltpu.make_async_copy(landed, landed, recv_sem.at[half]).wait()
        for a, spec in ((0, mixed_s), (1, gated_s)):
            block = jnp.concatenate([recv[holder[j], a * part:(a + 1) * part, :] for j in range(n)], axis=0)
            spec[...] = jnp.dot(block, fwd_ref[...], preferred_element_type=f32).reshape(n, part, 2 * rows)
        block = jnp.concatenate([recv[j, 2 * part:3 * part, :] for j in range(n)], axis=0)
        taps_spec = jnp.dot(block, fwd_ref[...], preferred_element_type=f32)
        before = jnp.concatenate([jnp.zeros((part, 2 * rows), f32), taps_spec[: (n - 1) * part]], axis=0)
        resp_s[...] = (before + wide_sign * taps_spec).reshape(n, part, 2 * rows)

        def tile(u, _):
            rws = pl.ds(pl.multiple_of(u * 8, 8), 8)
            zero = jnp.zeros((8, 128), f32)

            acc = [zero] * (2 * n)
            for k in range(n):
                rr, ri = resp_s[k, rws, re], resp_s[k, rws, im]
                ri0, rr2 = jnp.where(first, 0.0, ri), jnp.where(first, ri, rr)
                for p in range(k, n):
                    mr, mi = mixed_s[p - k, rws, re], mixed_s[p - k, rws, im]
                    acc[2 * p] += mr * rr - mi * ri0
                    acc[2 * p + 1] += mr * ri0 + mi * rr2
            for p in range(n):
                sum_s[p, rws, re] = acc[2 * p]
                sum_s[p, rws, im] = acc[2 * p + 1]

            acc = [zero] * (2 * n)
            for k in range(n):
                rr, ri = resp_s[k, rws, re], resp_s[k, rws, im]
                ri0, rr2 = jnp.where(first, 0.0, ri), jnp.where(first, ri, rr)
                for r in range(n - k):
                    gr, gi = gated_s[r + k, rws, re], gated_s[r + k, rws, im]
                    acc[2 * r] += gr * rr + gi * ri0
                    acc[2 * r + 1] += gi * rr2 - gr * ri0
            for r in range(n):
                sum_g[r, rws, re] = acc[2 * r]
                sum_g[r, rws, im] = acc[2 * r + 1]

            acc = [zero] * (2 * n)
            for r in range(n):
                mr, mi = mixed_s[r, rws, re], mixed_s[r, rws, im]
                mi0, mr2 = jnp.where(first, 0.0, mi), jnp.where(first, -mi, mr)
                for k in range(n - r):
                    gr, gi = gated_s[r + k, rws, re], gated_s[r + k, rws, im]
                    acc[2 * k] += mr * gr + mi0 * gi
                    acc[2 * k + 1] += mi0 * gr - mr2 * gi
            for k in range(n):
                for c, at in ((0, re), (1, im)):
                    own_sum = acc[2 * k + c]
                    if k + 1 < n:
                        own_sum = own_sum + sign * acc[2 * k + 2 + c]
                    sum_f[k, rws, at] = own_sum
            return 0

        lax.fori_loop(0, part // 8, tile, 0)

        for a, (sums, table) in enumerate(((sum_s, out_tab_ref), (sum_g, out_tab_ref), (sum_f, lag_tab_ref))):
            place = order if a < 2 else list(range(n))
            block = jnp.concatenate([sums[place[p]].astype(bf16) for p in range(n)], axis=0)
            turned = jnp.dot(block, table[...], preferred_element_type=f32)
            if a == 2:
                turned = turned * scale
            send_out[half, :, a * part:(a + 1) * part, :] = turned.astype(bf16).reshape(n, part, rows)
        for hop in hops:
            peer = peer_of(hop)
            pltpu.make_async_remote_copy(
                src_ref=send_out.at[half, peer], dst_ref=back.at[half, me],
                send_sem=back_send, recv_sem=back_recv,
                device_id={"seq": peer}, device_id_type=MESH,
            ).start()
        back[half, me] = send_out[half, me]

    landed = back.at[:, pl.ds(0, n - 1)]
    pltpu.make_async_copy(landed, landed, back_recv).wait()

    for g in range(channels // 128):
        cols = slice(g * 128, (g + 1) * 128)
        turned = []
        for a in range(3):
            pieces = []
            for i in range(128 // part):
                peer, half = (g * 128 + i * part) // own, i % HALVES
                pieces.append(back[half, peer, a * part:(a + 1) * part, :])
            turned.append(jnp.concatenate(pieces, axis=0).astype(f32).T)
        q, k, v, o = q_ref[:, cols], k_ref[:, cols], v_ref[:, cols], o_ref[:, cols]
        gain = gain_ref[:, cols]
        conv_out = turned[0] + gain * (k * v).astype(bf16).astype(f32)
        conv_grad = turned[1] + gain * (o * q).astype(bf16).astype(f32)
        hyena_ref[:, cols] = (q * conv_out).astype(bf16)
        gq_ref[:, cols] = (o * conv_out).astype(bf16)
        gk_ref[:, cols] = (conv_grad * v).astype(bf16)
        gv_ref[:, cols] = (conv_grad * k).astype(bf16)
        gf_ref[:, cols] = turned[2].astype(bf16)

    sent = send_in.at[:, pl.ds(0, n - 1)]
    pltpu.make_async_copy(sent, sent, send_sem).wait()
    sent = send_out.at[:, pl.ds(0, n - 1)]
    pltpu.make_async_copy(sent, sent, back_send).wait()


def on_device(query_proj, key_proj, value_proj, filter_taps, skip_gain, out_grad, block_order):
    n = lax.axis_size("seq")
    rows, channels = query_proj.shape
    part = channels // n // HALVES
    bf16, f32 = jnp.bfloat16, jnp.float32
    vmem = pl.BlockSpec(memory_space=pltpu.VMEM)
    tables = spectrum_tables(rows)
    spec = pltpu.VMEM((n, part, 2 * rows), f32)
    message = (HALVES, n, 3 * part, rows)
    return pl.pallas_call(
        functools.partial(kernel, n),
        out_shape=[jax.ShapeDtypeStruct((rows, channels), bf16)] * 5,
        in_specs=[vmem] * 6 + [pl.BlockSpec(memory_space=pltpu.SMEM)] + [vmem] * 3,
        out_specs=[vmem] * 5,
        scratch_shapes=[
            pltpu.VMEM(message, bf16),
            pltpu.VMEM(message[1:], bf16),
            pltpu.VMEM(message[1:], bf16),
            pltpu.VMEM(message, bf16),
            pltpu.VMEM(message, bf16),
            spec, spec, spec, spec, spec, spec,
            pltpu.SemaphoreType.DMA(()),
            pltpu.SemaphoreType.DMA((HALVES,)),
            pltpu.SemaphoreType.DMA(()),
            pltpu.SemaphoreType.DMA(()),
        ],
        compiler_params=pltpu.CompilerParams(
            collective_id=0, has_side_effects=True, vmem_limit_bytes=32 * 2**20
        ),
    )(
        query_proj, key_proj, value_proj, out_grad, filter_taps, skip_gain[None, :], block_order,
        *[jnp.asarray(t) for t in tables],
    )


def solution(mesh):
    placed = (
        P(("dp", "seq"), "chan"),
        P(("dp", "seq"), "chan"),
        P(("dp", "seq"), "chan"),
        P("seq", "chan"),
        P("chan"),
        P(("dp", "seq"), "chan"),
        P("dp"),
    )
    return jax.shard_map(
        on_device,
        mesh=mesh,
        in_specs=placed,
        out_specs=(P(("dp", "seq"), "chan"),) * 5,
        check_vma=False,
    )
```

time: 654 us -> 43.5 us (0.07)
  waiting for transfers between devices: 348 us -> 0 us
  other arithmetic: 108 us -> 0 us
  matrix products: 87 us -> 0 us
  local copies, waits for them, and re-layouts: 72.3 us -> 11.9 us
  Pallas kernels: 0 us -> 30.6 us
  loops' own time: 19.9 us -> 0 us
  between operations: 14.2 us -> 0.66 us
    reduce_scatter x1 -> x0, waiting for transfers between devices: 197 us -> none  [on_device(): lax.psum_scatter(partial_value[block_rows:], 'seq', scatter_dimension=0,...]
    dot_general x81 -> x0, matrix products: 87 us -> none  [the longest x31 38.6 us: window(): return jnp.dot(full_table, window_rows, preferred_element_type=jnp.float32)]
    all_gather x1 -> x0, waiting for transfers between devices: 81.2 us -> none  [on_device(): every_tap = lax.all_gather(scaled_taps, 'seq', axis=0, tiled=True)]
    ppermute x15 -> x0, waiting for transfers between devices: 69.7 us -> none  [from_behind(): lax.ppermute(array, axis, [(i, (i + by) % peers) for i in range(peers)])]
    add x16 -> x0, other arithmetic: 51.5 us -> none  [the longest x15 51.5 us: visit(): out_spec + ahead_mask * complex_mul(mixed_spec, window(ahead_lag))]
    another operation x19 -> x0, other arithmetic: 41.2 us -> none
    pallas_call x0 -> x1, Pallas kernels: none -> 30.6 us  [on_device(): pl.pallas_call(functools.partial(kernel, n), out_shape=[jax.ShapeDtypeStr...]
    dynamic_slice x46 -> x0, local copies, waits for them, and re-layouts: 30.4 us -> none  [the longest x30 19.2 us: visit(): lax.dynamic_slice_in_dim(partial_value, offset, spectrum_length, 0)]
  transfers between devices with their start and end apart: 17 -> 0, of which waited for: 17 -> 0; matrix products, arithmetic and copies ran while one was open for 13% -> 0% of each run, Pallas kernels for 0% -> 0%
where the time goes in v1:
time: 43.5 us; the launch traced here: 43.1 us
  Pallas kernels  30.6 us (70%)
  local copies, waits for them, and re-layouts  11.9 us (27%)
  between operations  0.66 us (2%)
    pallas_call x1, Pallas kernels, on_device(): pl.pallas_call(functools.partial(kernel, n), out_shape=[jax.ShapeDtypeStr...  30.6 us
    unnamed x25, local copies, waits for them, and re-layouts  11.9 us

profile of v1, /device:TPU:8, one launch (start us, length us, event | category | flops | bytes accessed | tf_op | source)
XLA Modules:
  0.0 43.1 jit_solution(8277221723161979889)
XLA Ops:
  0.6 0.0 copy-start.9
  0.6 0.6 %copy-done.9 = s32[16]{0:T(128)S(1)} copy-done((s32[16]{0:T(128)S(1)}, s32[16]{0:T(128)}, u32[]{:S(2)}) %copy-start.9) | copy-done | bytes 88
  1.3 0.0 copy-start
  1.3 0.9 %copy-done = f32[128,512]{1,0:T(8,128)S(1)} copy-done((f32[128,512]{1,0:T(8,128)S(1)}, f32[128,512]{1,0:T(8,128)}, u32[]{:S(2)}) %copy-start) | copy-done | bytes 262168
  2.2 0.0 copy-start.1
  2.2 0.9 %copy-done.1 = f32[128,512]{1,0:T(8,128)S(1)} copy-done((f32[128,512]{1,0:T(8,128)S(1)}, f32[128,512]{1,0:T(8,128)}, u32[]{:S(2)}) %copy-start.1) | copy-done | bytes 262168
  3.2 0.0 copy-start.2
  3.2 0.9 %copy-done.2 = f32[128,512]{1,0:T(8,128)S(1)} copy-done((f32[128,512]{1,0:T(8,128)S(1)}, f32[128,512]{1,0:T(8,128)}, u32[]{:S(2)}) %copy-start.2) | copy-done | bytes 262168
  4.1 0.0 copy-start.3
  4.1 0.9 %copy-done.3 = f32[128,512]{1,0:T(8,128)S(1)} copy-done((f32[128,512]{1,0:T(8,128)S(1)}, f32[128,512]{1,0:T(8,128)}, u32[]{:S(2)}) %copy-start.3) | copy-done | bytes 262168
  5.1 0.0 copy-start.4
  5.1 0.9 %copy-done.4 = f32[128,512]{1,0:T(8,128)S(1)} copy-done((f32[128,512]{1,0:T(8,128)S(1)}, f32[128,512]{1,0:T(8,128)}, u32[]{:S(2)}) %copy-start.4) | copy-done | bytes 262168
  6.0 0.0 copy-start.5
  6.0 0.8 %copy-done.5 = bf16[256,128]{1,0:T(8,128)(2,1)S(1)} copy-done((bf16[256,128]{1,0:T(8,128)(2,1)S(1)}, bf16[256,128]{1,0:T(8,128)(2,1)}, u32[]{:S(2)}) %copy-start.5) | copy-done | bytes 65560
  6.9 0.0 copy-start.6
  6.9 0.8 %copy-done.6 = bf16[256,128]{1,0:T(8,128)(2,1)S(1)} copy-done((bf16[256,128]{1,0:T(8,128)(2,1)S(1)}, bf16[256,128]{1,0:T(8,128)(2,1)}, u32[]{:S(2)}) %copy-start.6) | copy-done | bytes 65560
  7.7 0.0 copy-start.7
  7.7 0.8 %copy-done.7 = bf16[128,256]{1,0:T(8,128)(2,1)S(1)} copy-done((bf16[128,256]{1,0:T(8,128)(2,1)S(1)}, bf16[128,256]{1,0:T(8,128)(2,1)}, u32[]{:S(2)}) %copy-start.7) | copy-done | bytes 65560
  8.6 0.0 copy-start.8
  8.6 0.7 %copy-done.8 = f32[512]{0:T(512)S(1)} copy-done((f32[512]{0:T(512)S(1)}, f32[512]{0:T(512)}, u32[]{:S(2)}) %copy-start.8) | copy-done | bytes 2072
  9.2 30.6 %shard_map.137 = (bf16[128,512]{1,0:T(8,128)(2,1)S(1)}, bf16[128,512]{1,0:T(8,128)(2,1)S(1)}, bf16[128,512]{1,0:T(8,128)(2,1)S(1)}, bf16[128,512]{1,0:T(8,128)(2,1)S(1)}, bf16[128,512]{1,0:T(8,128)(2,1)S(1)}) custom-call(f32[128,512]{1,0:T(8,128)S(1)} %copy-done, f32[128,512]{1,0:T(8,128)S(1)} %copy-done.1, f32[128,512]{1,0:T(8,128)S(1)} %copy-done.2, ...), custom_call_target="tpu_custom_call" | custom-call | tf_op jit(solution)/shard_map/pallas_call | solution.py:211
  39.8 0.7 %copy.20 = bf16[128,512]{1,0:T(8,128)(2,1)} copy(bf16[128,512]{1,0:T(8,128)(2,1)S(1)} %get-tuple-element.10) | data formatting | bytes 262144
  40.5 0.7 %copy.21 = bf16[128,512]{1,0:T(8,128)(2,1)} copy(bf16[128,512]{1,0:T(8,128)(2,1)S(1)} %get-tuple-element.11) | data formatting | bytes 262144
  41.1 0.7 %copy.22 = bf16[128,512]{1,0:T(8,128)(2,1)} copy(bf16[128,512]{1,0:T(8,128)(2,1)S(1)} %get-tuple-element.12) | data formatting | bytes 262144
  41.8 0.7 %copy.23 = bf16[128,512]{1,0:T(8,128)(2,1)} copy(bf16[128,512]{1,0:T(8,128)(2,1)S(1)} %get-tuple-element.13) | data formatting | bytes 262144
  42.5 0.7 %copy.24 = bf16[128,512]{1,0:T(8,128)(2,1)} copy(bf16[128,512]{1,0:T(8,128)(2,1)S(1)} %get-tuple-element.14) | data formatting | bytes 262144
Async XLA Ops:
  0.6 0.7 %copy-start.9 = (s32[16]{0:T(128)S(1)}, s32[16]{0:T(128)}, u32[]{:S(2)}) copy-start(s32[16]{0:T(128)} %order_ref.1) | copy-start | bytes 196
  1.3 0.9 %copy-start = (f32[128,512]{1,0:T(8,128)S(1)}, f32[128,512]{1,0:T(8,128)}, u32[]{:S(2)}) copy-start(f32[128,512]{1,0:T(8,128)} %q_ref.1) | copy-start | bytes 786436
  2.2 0.9 %copy-start.1 = (f32[128,512]{1,0:T(8,128)S(1)}, f32[128,512]{1,0:T(8,128)}, u32[]{:S(2)}) copy-start(f32[128,512]{1,0:T(8,128)} %k_ref.1) | copy-start | bytes 786436
  3.2 0.9 %copy-start.2 = (f32[128,512]{1,0:T(8,128)S(1)}, f32[128,512]{1,0:T(8,128)}, u32[]{:S(2)}) copy-start(f32[128,512]{1,0:T(8,128)} %v_ref.1) | copy-start | bytes 786436
  4.1 0.9 %copy-start.3 = (f32[128,512]{1,0:T(8,128)S(1)}, f32[128,512]{1,0:T(8,128)}, u32[]{:S(2)}) copy-start(f32[128,512]{1,0:T(8,128)} %o_ref.1) | copy-start | bytes 786436
  5.1 0.9 %copy-start.4 = (f32[128,512]{1,0:T(8,128)S(1)}, f32[128,512]{1,0:T(8,128)}, u32[]{:S(2)}) copy-start(f32[128,512]{1,0:T(8,128)} %taps_ref.1) | copy-start | bytes 786436
  6.0 0.8 %copy-start.5 = (bf16[256,128]{1,0:T(8,128)(2,1)S(1)}, bf16[256,128]{1,0:T(8,128)(2,1)}, u32[]{:S(2)}) copy-start(bf16[256,128]{1,0:T(8,128)(2,1)} %constant.8.clone.lag_tab_ref) | copy-start | bytes 196612
  6.9 0.8 %copy-start.6 = (bf16[256,128]{1,0:T(8,128)(2,1)S(1)}, bf16[256,128]{1,0:T(8,128)(2,1)}, u32[]{:S(2)}) copy-start(bf16[256,128]{1,0:T(8,128)(2,1)} %constant.7.clone.out_tab_ref) | copy-start | bytes 196612
  7.7 0.8 %copy-start.7 = (bf16[128,256]{1,0:T(8,128)(2,1)S(1)}, bf16[128,256]{1,0:T(8,128)(2,1)}, u32[]{:S(2)}) copy-start(bf16[128,256]{1,0:T(8,128)(2,1)} %constant.6.clone.fwd_ref) | copy-start | bytes 196612
  8.6 0.7 %copy-start.8 = (f32[512]{0:T(512)S(1)}, f32[512]{0:T(512)}, u32[]{:S(2)}) copy-start(f32[512]{0:T(512)} %param.14) | copy-start | bytes 6148

commit v2 on v1

--- a/solution.py
+++ b/solution.py
@@ -27,14 +27,15 @@
     output = np.concatenate([weight * sign * np.cos(angle), weight * sign * sine], axis=1).T
     lag_sine = np.where(freq == 0, middle, np.sin(angle))
     lags = np.concatenate([weight * np.cos(angle), weight * lag_sine], axis=1).T
-    return [t.astype(ml_dtypes.bfloat16) for t in (forward, output, lags)]
-
-
-def kernel(
-    n, q_ref, k_ref, v_ref, o_ref, taps_ref, gain_ref, order_ref, fwd_ref, out_tab_ref, lag_tab_ref,
-    hyena_ref, gq_ref, gk_ref, gv_ref, gf_ref,
-    send_in, recv_a, recv_b, send_out, back, mixed_s, gated_s, resp_s, sum_s, sum_g, sum_f,
-    send_sem, recv_sem, back_send, back_recv,
+    stacked = np.concatenate([forward[:, :rows], forward[:, rows:], output, lags], axis=0)
+    return stacked.astype(ml_dtypes.bfloat16)
+
+
+def exchange_kernel(
+    n, q_hbm, k_hbm, v_hbm, o_hbm, taps_hbm, gain_hbm, order_hbm, tables_hbm,
+    back, q_ref, k_ref, v_ref, o_ref, gain_ref,
+    taps_ref, order_ref, tables, send_in, recv_a, recv_b, send_out, mixed_s, gated_s, resp_s, sum_s, sum_g, sum_f,
+    load_sem, send_sem, recv_sem, back_send, back_recv,
 ):
     me = lax.axis_index("seq")
     rows, channels = q_ref.shape
@@ -43,11 +44,23 @@
     scale = 1.0 / math.sqrt(rows * n)
     bf16, f32 = jnp.bfloat16, jnp.float32
 
+    loads = [
+        pltpu.make_async_copy(src, dst, load_sem.at[i])
+        for i, (src, dst) in enumerate((
+            (k_hbm, k_ref), (v_hbm, v_ref), (o_hbm, o_ref), (q_hbm, q_ref), (taps_hbm, taps_ref),
+            (tables_hbm, tables), (order_hbm, order_ref), (gain_hbm, gain_ref),
+        ))
+    ]
+    for load in loads:
+        load.start()
+
     barrier = pltpu.get_barrier_semaphore()
     for step in range(1, n):
         pl.semaphore_signal(barrier, inc=1, device_id={"seq": lax.rem(me + step, n)}, device_id_type=MESH)
 
     for a in range(3):
+        for load in loads[2 * a : 2 * a + 2] if a < 2 else loads[4:5]:
+            load.wait()
         for g in range(channels // 128):
             cols = slice(g * 128, (g + 1) * 128)
             if a == 0:
@@ -82,6 +95,11 @@
     for half in range(HALVES):
         recvs[half][me] = send_in[half, me]
 
+    for load in loads[5:]:
+        load.wait()
+    fwd = jnp.concatenate([tables[0:rows], tables[rows : 2 * rows]], axis=1)
+    out_tab, lag_tab = tables[2 * rows : 4 * rows], tables[4 * rows : 6 * rows]
+
     order = [order_ref[p] for p in range(n)]
     holder = []
     for j in range(n):
@@ -103,9 +121,9 @@
         pltpu.make_async_copy(landed, landed, recv_sem.at[half]).wait()
         for a, spec in ((0, mixed_s), (1, gated_s)):
             block = jnp.concatenate([recv[holder[j], a * part:(a + 1) * part, :] for j in range(n)], axis=0)
-            spec[...] = jnp.dot(block, fwd_ref[...], preferred_element_type=f32).reshape(n, part, 2 * rows)
+            spec[...] = jnp.dot(block, fwd, preferred_element_type=f32).reshape(n, part, 2 * rows)
         block = jnp.concatenate([recv[j, 2 * part:3 * part, :] for j in range(n)], axis=0)
-        taps_spec = jnp.dot(block, fwd_ref[...], preferred_element_type=f32)
+        taps_spec = jnp.dot(block, fwd, preferred_element_type=f32)
         before = jnp.concatenate([jnp.zeros((part, 2 * rows), f32), taps_spec[: (n - 1) * part]], axis=0)
         resp_s[...] = (before + wide_sign * taps_spec).reshape(n, part, 2 * rows)
 
@@ -155,10 +173,10 @@
 
         lax.fori_loop(0, part // 8, tile, 0)
 
-        for a, (sums, table) in enumerate(((sum_s, out_tab_ref), (sum_g, out_tab_ref), (sum_f, lag_tab_ref))):
+        for a, (sums, table) in enumerate(((sum_s, out_tab), (sum_g, out_tab), (sum_f, lag_tab))):
             place = order if a < 2 else list(range(n))
             block = jnp.concatenate([sums[place[p]].astype(bf16) for p in range(n)], axis=0)
-            turned = jnp.dot(block, table[...], preferred_element_type=f32)
+            turned = jnp.dot(block, table, preferred_element_type=f32)
             if a == 2:
                 turned = turned * scale
             send_out[half, :, a * part:(a + 1) * part, :] = turned.astype(bf16).reshape(n, part, rows)
@@ -174,6 +192,21 @@
     landed = back.at[:, pl.ds(0, n - 1)]
     pltpu.make_async_copy(landed, landed, back_recv).wait()
 
+    sent = send_in.at[:, pl.ds(0, n - 1)]
+    pltpu.make_async_copy(sent, sent, send_sem).wait()
+    sent = send_out.at[:, pl.ds(0, n - 1)]
+    pltpu.make_async_copy(sent, sent, back_send).wait()
+
+
+def gate_kernel(
+    n, back, q_ref, k_ref, v_ref, o_ref, gain_ref, hyena_hbm, gq_hbm, gk_hbm, gv_hbm, gf_hbm, results, sems
+):
+    rows, channels = q_ref.shape
+    own = channels // n
+    part = own // HALVES
+    bf16, f32 = jnp.bfloat16, jnp.float32
+    outs = (hyena_hbm, gq_hbm, gk_hbm, gv_hbm, gf_hbm)
+    stores = []
     for g in range(channels // 128):
         cols = slice(g * 128, (g + 1) * 128)
         turned = []
@@ -181,22 +214,20 @@
             pieces = []
             for i in range(128 // part):
                 peer, half = (g * 128 + i * part) // own, i % HALVES
-                pieces.append(back[half, peer, a * part:(a + 1) * part, :])
+                pieces.append(back[half, peer, a * part : (a + 1) * part, :])
             turned.append(jnp.concatenate(pieces, axis=0).astype(f32).T)
         q, k, v, o = q_ref[:, cols], k_ref[:, cols], v_ref[:, cols], o_ref[:, cols]
         gain = gain_ref[:, cols]
         conv_out = turned[0] + gain * (k * v).astype(bf16).astype(f32)
         conv_grad = turned[1] + gain * (o * q).astype(bf16).astype(f32)
-        hyena_ref[:, cols] = (q * conv_out).astype(bf16)
-        gq_ref[:, cols] = (o * conv_out).astype(bf16)
-        gk_ref[:, cols] = (conv_grad * v).astype(bf16)
-        gv_ref[:, cols] = (conv_grad * k).astype(bf16)
-        gf_ref[:, cols] = turned[2].astype(bf16)
-
-    sent = send_in.at[:, pl.ds(0, n - 1)]
-    pltpu.make_async_copy(sent, sent, send_sem).wait()
-    sent = send_out.at[:, pl.ds(0, n - 1)]
-    pltpu.make_async_copy(sent, sent, back_send).wait()
+        values = (q * conv_out, o * conv_out, conv_grad * v, conv_grad * k, turned[2])
+        for i, value in enumerate(values):
+            results[i, :, cols] = value.astype(bf16)
+            store = pltpu.make_async_copy(results.at[i, :, cols], outs[i].at[:, cols], sems.at[i, g])
+            store.start()
+            stores.append(store)
+    for store in stores:
+        store.wait()
 
 
 def on_device(query_proj, key_proj, value_proj, filter_taps, skip_gain, out_grad, block_order):
@@ -205,21 +236,26 @@
     part = channels // n // HALVES
     bf16, f32 = jnp.bfloat16, jnp.float32
     vmem = pl.BlockSpec(memory_space=pltpu.VMEM)
-    tables = spectrum_tables(rows)
+    hbm = pl.BlockSpec(memory_space=pltpu.HBM)
     spec = pltpu.VMEM((n, part, 2 * rows), f32)
     message = (HALVES, n, 3 * part, rows)
-    return pl.pallas_call(
-        functools.partial(kernel, n),
-        out_shape=[jax.ShapeDtypeStruct((rows, channels), bf16)] * 5,
-        in_specs=[vmem] * 6 + [pl.BlockSpec(memory_space=pltpu.SMEM)] + [vmem] * 3,
-        out_specs=[vmem] * 5,
+    block = jax.ShapeDtypeStruct((rows, channels), f32)
+    tables = spectrum_tables(rows)
+    kept = pl.pallas_call(
+        functools.partial(exchange_kernel, n),
+        out_shape=[jax.ShapeDtypeStruct(message, bf16)] + [block] * 4 + [jax.ShapeDtypeStruct((1, channels), f32)],
+        in_specs=[hbm] * 8,
+        out_specs=[vmem] * 6,
         scratch_shapes=[
+            pltpu.VMEM((rows, channels), f32),
+            pltpu.SMEM((n,), jnp.int32),
+            pltpu.VMEM(tables.shape, bf16),
             pltpu.VMEM(message, bf16),
             pltpu.VMEM(message[1:], bf16),
             pltpu.VMEM(message[1:], bf16),
             pltpu.VMEM(message, bf16),
-            pltpu.VMEM(message, bf16),
             spec, spec, spec, spec, spec, spec,
+            pltpu.SemaphoreType.DMA((8,)),
             pltpu.SemaphoreType.DMA(()),
             pltpu.SemaphoreType.DMA((HALVES,)),
             pltpu.SemaphoreType.DMA(()),
@@ -228,10 +264,27 @@
         compiler_params=pltpu.CompilerParams(
             collective_id=0, has_side_effects=True, vmem_limit_bytes=32 * 2**20
         ),
-    )(
-        query_proj, key_proj, value_proj, out_grad, filter_taps, skip_gain[None, :], block_order,
-        *[jnp.asarray(t) for t in tables],
-    )
+        name="exchange",
+    )(*[
+        pltpu.with_memory_space_constraint(x, pltpu.HBM)
+        for x in (
+            query_proj, key_proj, value_proj, out_grad, filter_taps, skip_gain[None, :], block_order,
+            jnp.asarray(tables),
+        )
+    ])
+    result = jax.ShapeDtypeStruct((rows, channels), bf16)
+    return pl.pallas_call(
+        functools.partial(gate_kernel, n),
+        out_shape=[result] * 5,
+        in_specs=[vmem] * 6,
+        out_specs=[hbm] * 5,
+        scratch_shapes=[
+            pltpu.VMEM((5, rows, channels), bf16),
+            pltpu.SemaphoreType.DMA((5, channels // 128)),
+        ],
+        compiler_params=pltpu.CompilerParams(vmem_limit_bytes=32 * 2**20),
+        name="gate",
+    )(*kept)
 
 
 def solution(mesh):

time: 43.5 us -> 31.9 us (0.73)
  local copies, waits for them, and re-layouts: 11.9 us -> 0 us
  Pallas kernels: 30.6 us -> 31.1 us
    unnamed x25 -> x0, local copies, waits for them, and re-layouts: 11.9 us -> none
    pallas_call x1 -> x2, Pallas kernels: 30.6 us -> 31.1 us  [the longest x1 30 us: on_device(): pl.pallas_call(functools.partial(exchange_kernel, n), out_shape=[jax.Shap...]
where the time goes in v2:
time: 31.9 us; the launch traced here: 31.8 us
  Pallas kernels  31.1 us (97%)
  between operations  0.64 us (2%)
    pallas_call x1, Pallas kernels, on_device(): pl.pallas_call(functools.partial(exchange_kernel, n), out_shape=[jax.Shap...  30 us
    pallas_call x1, Pallas kernels, on_device(): pl.pallas_call(functools.partial(gate_kernel, n), out_shape=[result] * 5,...  1.11 us

profile of v2, /device:TPU:8, one launch (start us, length us, event | category | flops | bytes accessed | tf_op | source)
XLA Modules:
  0.0 31.8 jit_solution(15155261745782143073)
XLA Ops:
  0.6 30.0 %exchange.1 = (bf16[2,16,48,128]{3,2,1,0:T(8,128)(2,1)S(1)}, f32[128,512]{1,0:T(8,128)S(1)}, f32[128,512]{1,0:T(8,128)S(1)}, f32[128,512]{1,0:T(8,128)S(1)}, f32...) custom-call(f32[128,512]{1,0:T(8,128)} %q_hbm.1, f32[128,512]{1,0:T(8,128)} %k_hbm.1, f32[128,512]{1,0:T(8,128)} %v_hbm.1, ...), custom_call_target="tpu_custom_call" | custom-call | tf_op jit(solution)/shard_map/exchange/pallas_call | solution.py:244
  30.6 1.1 %gate.1 = (bf16[128,512]{1,0:T(8,128)(2,1)}, bf16[128,512]{1,0:T(8,128)(2,1)}, bf16[128,512]{1,0:T(8,128)(2,1)}, bf16[128,512]{1,0:T(8,128)(2,1)}, bf16[128,512]{1,0:T(8,128)(2,1)}) custom-call(bf16[2,16,48,128]{3,2,1,0:T(8,128)(2,1)S(1)} %get-tuple-element.11.back, f32[128,512]{1,0:T(8,128)S(1)} %get-tuple-element.12.q_ref, ...), custom_call_target="tpu_custom_call" | custom-call | tf_op jit(solution)/shard_map/gate/pallas_call | solution.py:276

commit v3 on v2

v3 whole, which is shorter than its diff:
```python
import functools
import math

import jax
import jax.numpy as jnp
import ml_dtypes
import numpy as np
from jax import lax
from jax.experimental import pallas as pl
from jax.experimental.pallas import tpu as pltpu
from jax.sharding import PartitionSpec as P

MESH = pl.DeviceIdType.MESH
HALVES = 2


def spectrum_tables(rows):
    length = 2 * rows
    time = np.arange(rows)[:, None]
    freq = np.arange(rows)[None, :]
    angle = 2.0 * np.pi / length * ((time * freq) % length)
    middle = 1.0 - 2.0 * (time % 2)
    sine = np.where(freq == 0, middle, -np.sin(angle))
    forward = np.concatenate([np.cos(angle), sine], axis=1)
    sign = 1.0 - 2.0 * (freq % 2)
    weight = np.where(freq == 0, 1.0, 2.0) / length
    output = np.concatenate([weight * sign * np.cos(angle), weight * sign * sine], axis=1).T
    lag_sine = np.where(freq == 0, middle, np.sin(angle))
    lags = np.concatenate([weight * np.cos(angle), weight * lag_sine], axis=1).T
    stacked = np.concatenate([forward[:, :rows], forward[:, rows:], output, lags], axis=0)
    return stacked.astype(ml_dtypes.bfloat16)


def exchange_kernel(
    n, q_hbm, k_hbm, v_hbm, o_hbm, taps_hbm, gain_hbm, order_hbm, tables_hbm,
    back, q_ref, k_ref, v_ref, o_ref, gain_ref,
    taps_ref, order_ref, tables, send_in, recv_tm, recv_g, recv_m2, recv_g2, recv_t2, send_out,
    mixed_s, gated_s, resp_s, sum_s, sum_f,
    load_sem, send_sem, recv_sem, pass_sem, back_send, back_recv,
):
    me, core = lax.axis_index("seq"), lax.axis_index("dp")
    rows, channels = q_ref.shape
    own = channels // n
    part = own // HALVES
    scale = 1.0 / math.sqrt(rows * n)
    bf16, f32 = jnp.bfloat16, jnp.float32

    barrier = pltpu.get_barrier_semaphore()
    for step in range(1, n):
        pl.semaphore_signal(barrier, inc=1, device_id={"seq": lax.rem(me + step, n)}, device_id_type=MESH)
    pl.semaphore_signal(barrier, inc=1, device_id={"dp": 1 - core}, device_id_type=MESH)

    loads = [
        pltpu.make_async_copy(src, dst, load_sem.at[i])
        for i, (src, dst) in enumerate((
            (taps_hbm, taps_ref), (k_hbm, k_ref), (v_hbm, v_ref), (o_hbm, o_ref), (q_hbm, q_ref),
            (tables_hbm, tables), (order_hbm, order_ref), (gain_hbm, gain_ref),
        ))
    ]
    for load in loads:
        load.start()

    def turn(a):
        for g in range(channels // 128):
            cols = slice(g * 128, (g + 1) * 128)
            if a == 0:
                block = taps_ref[:, cols] * scale
            elif a == 1:
                block = k_ref[:, cols] * v_ref[:, cols]
            else:
                block = o_ref[:, cols] * q_ref[:, cols]
            turned = block.T.astype(bf16)
            for i in range(128 // part):
                peer, half = (g * 128 + i * part) // own, i % HALVES
                send_in[half, peer, a * part : (a + 1) * part, :] = turned[i * part : (i + 1) * part]

    hops = [(h, z) for z in (4, 3, 5, 2, 6, 1, 7, 0) for h in (1, 0) if (h, z) != (0, 0)]

    def send_all(source, target, send, recv):
        ring = n // 2
        for h, z in hops:
            peer = lax.rem(me // ring + h, 2) * ring + lax.rem(me + z, ring)
            pltpu.make_async_remote_copy(
                src_ref=source(peer), dst_ref=target, send_sem=send, recv_sem=recv,
                device_id={"seq": peer}, device_id_type=MESH,
            ).start()

    early, late = core, 1 - core
    inputs = (
        (early, 0, 2 * part, recv_tm), (early, 2 * part, part, recv_g),
        (late, part, part, recv_m2), (late, 2 * part, part, recv_g2),
    )

    def send_input(i):
        half, start, size, recv = inputs[i]
        rws = pl.ds(start, size)
        send_all(lambda peer: send_in.at[half, peer, rws], recv.at[me], send_sem, recv_sem.at[i])
        recv[me] = send_in[half, me, rws, :]

    def wait_input(i):
        landed = inputs[i][3].at[pl.ds(0, n - 1)]
        pltpu.make_async_copy(landed, landed, recv_sem.at[i]).wait()

    loads[0].wait()
    turn(0)
    loads[1].wait()
    loads[2].wait()
    turn(1)
    pl.semaphore_wait(barrier, n)
    send_input(0)
    loads[3].wait()
    loads[4].wait()
    turn(2)
    for i in range(1, 4):
        send_input(i)

    for load in loads[5:]:
        load.wait()
    fwd = jnp.concatenate([tables[0:rows], tables[rows : 2 * rows]], axis=1)
    out_tab, lag_tab = tables[2 * rows : 4 * rows], tables[4 * rows : 6 * rows]

    order = [order_ref[p] for p in range(n)]
    holder = []
    for j in range(n):
        at = jnp.int32(0)
        for p in range(1, n):
            at = jnp.where(order[p] == j, p, at)
        holder.append(at)
    plain = list(range(n))

    lane = lax.broadcasted_iota(jnp.int32, (8, 128), 1)
    first = lane == 0
    sign = jnp.where(lane % 2 == 0, 1.0, -1.0).astype(f32)
    wide_lane = lax.broadcasted_iota(jnp.int32, (n * part, 2 * rows), 1)
    wide_sign = jnp.where(wide_lane % 2 == 0, 1.0, -1.0).astype(f32)
    re, im = slice(0, 128), slice(128, 256)
    zero = jnp.zeros((8, 128), f32)

    def spectra(recv, start, places):
        block = jnp.concatenate([recv[places[j], start : start + part, :] for j in range(n)], axis=0)
        return jnp.dot(block, fwd, preferred_element_type=f32)

    def response(recv):
        taps_spec = spectra(recv, 0, plain)
        before = jnp.concatenate([jnp.zeros((part, 2 * rows), f32), taps_spec[: (n - 1) * part]], axis=0)
        resp_s[...] = (before + wide_sign * taps_spec).reshape(n, part, 2 * rows)

    def tiles(body):
        def step(u, _):
            body(pl.ds(pl.multiple_of(u * 8, 8), 8))
            return 0

        lax.fori_loop(0, part // 8, step, 0)

    def forward_tile(rws):
        acc = [zero] * (2 * n)
        for k in range(n):
            rr, ri = resp_s[k, rws, re], resp_s[k, rws, im]
            ri0, rr2 = jnp.where(first, 0.0, ri), jnp.where(first, ri, rr)
            for p in range(k, n):
                mr, mi = mixed_s[p - k, rws, re], mixed_s[p - k, rws, im]
                acc[2 * p] += mr * rr - mi * ri0
                acc[2 * p + 1] += mr * ri0 + mi * rr2
        for p in range(n):
            sum_s[p, rws, re] = acc[2 * p]
            sum_s[p, rws, im] = acc[2 * p + 1]

    def backward_tile(rws):
        acc = [zero] * (2 * n)
        for k in range(n):
            rr, ri = resp_s[k, rws, re], resp_s[k, rws, im]
            ri0, rr2 = jnp.where(first, 0.0, ri), jnp.where(first, ri, rr)
            for r in range(n - k):
                gr, gi = gated_s[r + k, rws, re], gated_s[r + k, rws, im]
                acc[2 * r] += gr * rr + gi * ri0
                acc[2 * r + 1] += gi * rr2 - gr * ri0
        for r in range(n):
            sum_s[r, rws, re] = acc[2 * r]
            sum_s[r, rws, im] = acc[2 * r + 1]

        acc = [zero] * (2 * n)
        for r in range(n):
            mr, mi = mixed_s[r, rws, re], mixed_s[r, rws, im]
            mi0, mr2 = jnp.where(first, 0.0, mi), jnp.where(first, -mi, mr)
            for k in range(n - r):
                gr, gi = gated_s[r + k, rws, re], gated_s[r + k, rws, im]
                acc[2 * k] += mr * gr + mi0 * gi
                acc[2 * k + 1] += mi0 * gr - mr2 * gi
        for k in range(n):
            for c, at in ((0, re), (1, im)):
                own_sum = acc[2 * k + c]
                if k + 1 < n:
                    own_sum = own_sum + sign * acc[2 * k + 2 + c]
                sum_f[k, rws, at] = own_sum

    def result(half, a, sums, table, places, factor=None):
        block = jnp.concatenate([sums[places[p]].astype(bf16) for p in range(n)], axis=0)
        values = jnp.dot(block, table, preferred_element_type=f32)
        if factor is not None:
            values = values * factor
        send_out[half, :, a * part : (a + 1) * part, :] = values.astype(bf16).reshape(n, part, rows)

    def send_result(half, start, size):
        rws = pl.ds(start, size)
        send_all(lambda peer: send_out.at[half, peer, rws], back.at[half, me, rws], back_send, back_recv)
        back[half, me, rws, :] = send_out[half, me, rws, :]

    def convolve(half, mixed_in, mixed_start, taps_in):
        response(taps_in)
        mixed_s[...] = spectra(mixed_in, mixed_start, holder).reshape(n, part, 2 * rows)
        tiles(forward_tile)
        result(half, 0, sum_s, out_tab, order)
        send_result(half, 0, part)

    def correlate(half, gated_in):
        gated_s[...] = spectra(gated_in, 0, holder).reshape(n, part, 2 * rows)
        tiles(backward_tile)
        result(half, 1, sum_s, out_tab, order)
        result(half, 2, sum_f, lag_tab, plain, scale)
        send_result(half, part, 2 * part)

    wait_input(0)
    pass_on = pltpu.make_async_remote_copy(
        src_ref=recv_tm.at[:, pl.ds(0, part)], dst_ref=recv_t2,
        send_sem=pass_sem.at[0], recv_sem=pass_sem.at[1],
        device_id={"dp": 1 - core}, device_id_type=MESH,
    )
    pass_on.start()
    convolve(early, recv_tm, part, recv_tm)
    wait_input(1)
    correlate(early, recv_g)
    pass_on.wait()
    wait_input(2)
    convolve(late, recv_m2, 0, recv_t2)
    wait_input(3)
    correlate(late, recv_g2)

    landed = back.at[:, pl.ds(0, n - 1)]
    pltpu.make_async_copy(landed, landed, back_recv).wait()
    for _, _, _, recv in inputs:
        sent = recv.at[pl.ds(0, n - 1)]
        pltpu.make_async_copy(sent, sent, send_sem).wait()
    sent = send_out.at[:, pl.ds(0, n - 1)]
    pltpu.make_async_copy(sent, sent, back_send).wait()


def gate_kernel(
    n, back, q_ref, k_ref, v_ref, o_ref, gain_ref, hyena_hbm, gq_hbm, gk_hbm, gv_hbm, gf_hbm, results, sems
):
    rows, channels = q_ref.shape
    own = channels // n
    part = own // HALVES
    bf16, f32 = jnp.bfloat16, jnp.float32
    outs = (hyena_hbm, gq_hbm, gk_hbm, gv_hbm, gf_hbm)
    stores = []
    for g in range(channels // 128):
        cols = slice(g * 128, (g + 1) * 128)
        turned = []
        for a in range(3):
            pieces = []
            for i in range(128 // part):
                peer, half = (g * 128 + i * part) // own, i % HALVES
                pieces.append(back[half, peer, a * part : (a + 1) * part, :])
            turned.append(jnp.concatenate(pieces, axis=0).astype(f32).T)
        q, k, v, o = q_ref[:, cols], k_ref[:, cols], v_ref[:, cols], o_ref[:, cols]
        gain = gain_ref[:, cols]
        conv_out = turned[0] + gain * (k * v).astype(bf16).astype(f32)
        conv_grad = turned[1] + gain * (o * q).astype(bf16).astype(f32)
        values = (q * conv_out, o * conv_out, conv_grad * v, conv_grad * k, turned[2])
        for i, value in enumerate(values):
            results[i, :, cols] = value.astype(bf16)
            store = pltpu.make_async_copy(results.at[i, :, cols], outs[i].at[:, cols], sems.at[i, g])
            store.start()
            stores.append(store)
    for store in stores:
        store.wait()


def on_device(query_proj, key_proj, value_proj, filter_taps, skip_gain, out_grad, block_order):
    n = lax.axis_size("seq")
    rows, channels = query_proj.shape
    part = channels // n // HALVES
    bf16, f32 = jnp.bfloat16, jnp.float32
    vmem = pl.BlockSpec(memory_space=pltpu.VMEM)
    hbm = pl.BlockSpec(memory_space=pltpu.HBM)
    spec = pltpu.VMEM((n, part, 2 * rows), f32)
    small = pltpu.VMEM((n, part, rows), bf16)
    message = (HALVES, n, 3 * part, rows)
    block = jax.ShapeDtypeStruct((rows, channels), f32)
    tables = spectrum_tables(rows)
    kept = pl.pallas_call(
        functools.partial(exchange_kernel, n),
        out_shape=[jax.ShapeDtypeStruct(message, bf16)] + [block] * 4 + [jax.ShapeDtypeStruct((1, channels), f32)],
        in_specs=[hbm] * 8,
        out_specs=[vmem] * 6,
        scratch_shapes=[
            pltpu.VMEM((rows, channels), f32),
            pltpu.SMEM((n,), jnp.int32),
            pltpu.VMEM(tables.shape, bf16),
            pltpu.VMEM(message, bf16),
            pltpu.VMEM((n, 2 * part, rows), bf16),
            small, small, small, small,
            pltpu.VMEM(message, bf16),
            spec, spec, spec, spec, spec,
            pltpu.SemaphoreType.DMA((8,)),
            pltpu.SemaphoreType.DMA(()),
            pltpu.SemaphoreType.DMA((4,)),
            pltpu.SemaphoreType.DMA((2,)),
            pltpu.SemaphoreType.DMA(()),
            pltpu.SemaphoreType.DMA(()),
        ],
        compiler_params=pltpu.CompilerParams(
            collective_id=0, has_side_effects=True, vmem_limit_bytes=32 * 2**20
        ),
        name="exchange",
    )(*[
        pltpu.with_memory_space_constraint(x, pltpu.HBM)
        for x in (
            query_proj, key_proj, value_proj, out_grad, filter_taps, skip_gain[None, :], block_order,
            jnp.asarray(tables),
        )
    ])
    result = jax.ShapeDtypeStruct((rows, channels), bf16)
    return pl.pallas_call(
        functools.partial(gate_kernel, n),
        out_shape=[result] * 5,
        in_specs=[vmem] * 6,
        out_specs=[hbm] * 5,
        scratch_shapes=[
            pltpu.VMEM((5, rows, channels), bf16),
            pltpu.SemaphoreType.DMA((5, channels // 128)),
        ],
        compiler_params=pltpu.CompilerParams(vmem_limit_bytes=32 * 2**20),
        name="gate",
    )(*kept)


def solution(mesh):
    placed = (
        P(("dp", "seq"), "chan"),
        P(("dp", "seq"), "chan"),
        P(("dp", "seq"), "chan"),
        P("seq", "chan"),
        P("chan"),
        P(("dp", "seq"), "chan"),
        P("dp"),
    )
    return jax.shard_map(
        on_device,
        mesh=mesh,
        in_specs=placed,
        out_specs=(P(("dp", "seq"), "chan"),) * 5,
        check_vma=False,
    )
```

time: 31.9 us -> 30.6 us (0.959)
  Pallas kernels: 31.1 us -> 29.9 us
    pallas_call x1, Pallas kernels: 30 us -> 28.8 us  [on_device(): pl.pallas_call(functools.partial(exchange_kernel, n), out_shape=[jax.Shap...]
where the time goes in v3:
time: 30.6 us; the launch traced here: 30.5 us
  Pallas kernels  29.9 us (98%)
  between operations  0.64 us (2%)
    pallas_call x1, Pallas kernels, on_device(): pl.pallas_call(functools.partial(exchange_kernel, n), out_shape=[jax.Shap...  28.8 us
    pallas_call x1, Pallas kernels, on_device(): pl.pallas_call(functools.partial(gate_kernel, n), out_shape=[result] * 5,...  1.11 us

profile of v3, /device:TPU:8, one launch (start us, length us, event | category | flops | bytes accessed | tf_op | source)
XLA Modules:
  0.0 30.5 jit_solution(8867667220915664812)
XLA Ops:
  0.6 28.8 %exchange.1 = (bf16[2,16,48,128]{3,2,1,0:T(8,128)(2,1)S(1)}, f32[128,512]{1,0:T(8,128)S(1)}, f32[128,512]{1,0:T(8,128)S(1)}, f32[128,512]{1,0:T(8,128)S(1)}, f32...) custom-call(f32[128,512]{1,0:T(8,128)} %q_hbm.1, f32[128,512]{1,0:T(8,128)} %k_hbm.1, f32[128,512]{1,0:T(8,128)} %v_hbm.1, ...), custom_call_target="tpu_custom_call" | custom-call | tf_op jit(solution)/shard_map/exchange/pallas_call | solution.py:291
  29.4 1.1 %gate.1 = (bf16[128,512]{1,0:T(8,128)(2,1)}, bf16[128,512]{1,0:T(8,128)(2,1)}, bf16[128,512]{1,0:T(8,128)(2,1)}, bf16[128,512]{1,0:T(8,128)(2,1)}, bf16[128,512]{1,0:T(8,128)(2,1)}) custom-call(bf16[2,16,48,128]{3,2,1,0:T(8,128)(2,1)S(1)} %get-tuple-element.11.back, f32[128,512]{1,0:T(8,128)S(1)} %get-tuple-element.12.q_ref, ...), custom_call_target="tpu_custom_call" | custom-call | tf_op jit(solution)/shard_map/gate/pallas_call | solution.py:324

commit v4 on v3

--- a/solution.py
+++ b/solution.py
@@ -74,12 +74,16 @@
                 peer, half = (g * 128 + i * part) // own, i % HALVES
                 send_in[half, peer, a * part : (a + 1) * part, :] = turned[i * part : (i + 1) * part]
 
-    hops = [(h, z) for z in (4, 3, 5, 2, 6, 1, 7, 0) for h in (1, 0) if (h, z) != (0, 0)]
-
-    def send_all(source, target, send, recv):
-        ring = n // 2
-        for h, z in hops:
-            peer = lax.rem(me // ring + h, 2) * ring + lax.rem(me + z, ring)
+    hops = [(h, z) for h in (1, 0) for z in (4, 3, 5, 2, 6, 1, 7, 0) if (h, z) != (0, 0)]
+
+    ring = n // 2
+    peers = {
+        (h, z): lax.rem(me // ring + h, 2) * ring + lax.rem(me + z, ring) for h, z in hops
+    }
+
+    def send_all(source, target, send, recv, group=None):
+        for hop in group or hops:
+            peer = peers[hop]
             pltpu.make_async_remote_copy(
                 src_ref=source(peer), dst_ref=target, send_sem=send, recv_sem=recv,
                 device_id={"seq": peer}, device_id_type=MESH,
@@ -88,14 +92,18 @@
     early, late = core, 1 - core
     inputs = (
         (early, 0, 2 * part, recv_tm), (early, 2 * part, part, recv_g),
-        (late, part, part, recv_m2), (late, 2 * part, part, recv_g2),
+        (late, part, 2 * part, recv_m2),
     )
 
-    def send_input(i):
+    far = [(h, z) for h, z in hops if 2 * h + min(z, 8 - z) >= 5]
+    near = [hop for hop in hops if hop not in far]
+
+    def send_input(i, group=None):
         half, start, size, recv = inputs[i]
         rws = pl.ds(start, size)
-        send_all(lambda peer: send_in.at[half, peer, rws], recv.at[me], send_sem, recv_sem.at[i])
-        recv[me] = send_in[half, me, rws, :]
+        send_all(lambda peer: send_in.at[half, peer, rws], recv.at[me], send_sem, recv_sem.at[i], group)
+        if group is not near:
+            recv[me] = send_in[half, me, rws, :]
 
     def wait_input(i):
         landed = inputs[i][3].at[pl.ds(0, n - 1)]
@@ -106,13 +114,14 @@
     loads[1].wait()
     loads[2].wait()
     turn(1)
-    pl.semaphore_wait(barrier, n)
-    send_input(0)
     loads[3].wait()
     loads[4].wait()
     turn(2)
-    for i in range(1, 4):
-        send_input(i)
+    pl.semaphore_wait(barrier, n)
+    for group in (far, near):
+        send_input(0, group)
+        send_input(1, group)
+    send_input(2)
 
     for load in loads[5:]:
         load.wait()
@@ -212,8 +221,8 @@
         result(half, 0, sum_s, out_tab, order)
         send_result(half, 0, part)
 
-    def correlate(half, gated_in):
-        gated_s[...] = spectra(gated_in, 0, holder).reshape(n, part, 2 * rows)
+    def correlate(half, gated_in, start=0):
+        gated_s[...] = spectra(gated_in, start, holder).reshape(n, part, 2 * rows)
         tiles(backward_tile)
         result(half, 1, sum_s, out_tab, order)
         result(half, 2, sum_f, lag_tab, plain, scale)
@@ -232,8 +241,7 @@
     pass_on.wait()
     wait_input(2)
     convolve(late, recv_m2, 0, recv_t2)
-    wait_input(3)
-    correlate(late, recv_g2)
+    correlate(late, recv_m2, part)
 
     landed = back.at[:, pl.ds(0, n - 1)]
     pltpu.make_async_copy(landed, landed, back_recv).wait()
@@ -299,7 +307,7 @@
             pltpu.VMEM(tables.shape, bf16),
             pltpu.VMEM(message, bf16),
             pltpu.VMEM((n, 2 * part, rows), bf16),
-            small, small, small, small,
+            small, pltpu.VMEM((n, 2 * part, rows), bf16), small, small,
             pltpu.VMEM(message, bf16),
             spec, spec, spec, spec, spec,
             pltpu.SemaphoreType.DMA((8,)),

time: 30.6 us -> 29.9 us (0.977)
  Pallas kernels: 29.9 us -> 29.2 us
    pallas_call x1, Pallas kernels: 28.8 us -> 28.1 us  [on_device(): pl.pallas_call(functools.partial(exchange_kernel, n), out_shape=[jax.Shap...]
where the time goes in v4:
time: 29.9 us; the launch traced here: 29.8 us
  Pallas kernels  29.2 us (98%)
  between operations  0.64 us (2%)
    pallas_call x1, Pallas kernels, on_device(): pl.pallas_call(functools.partial(exchange_kernel, n), out_shape=[jax.Shap...  28.1 us
    pallas_call x1, Pallas kernels, on_device(): pl.pallas_call(functools.partial(gate_kernel, n), out_shape=[result] * 5,...  1.11 us

profile of v4, /device:TPU:8, one launch (start us, length us, event | category | flops | bytes accessed | tf_op | source)
XLA Modules:
  0.0 29.8 jit_solution(2339692170434412738)
XLA Ops:
  0.6 28.1 %exchange.1 = (bf16[2,16,48,128]{3,2,1,0:T(8,128)(2,1)S(1)}, f32[128,512]{1,0:T(8,128)S(1)}, f32[128,512]{1,0:T(8,128)S(1)}, f32[128,512]{1,0:T(8,128)S(1)}, f32...) custom-call(f32[128,512]{1,0:T(8,128)} %q_hbm.1, f32[128,512]{1,0:T(8,128)} %k_hbm.1, f32[128,512]{1,0:T(8,128)} %v_hbm.1, ...), custom_call_target="tpu_custom_call" | custom-call | tf_op jit(solution)/shard_map/exchange/pallas_call | solution.py:299
  28.7 1.1 %gate.1 = (bf16[128,512]{1,0:T(8,128)(2,1)}, bf16[128,512]{1,0:T(8,128)(2,1)}, bf16[128,512]{1,0:T(8,128)(2,1)}, bf16[128,512]{1,0:T(8,128)(2,1)}, bf16[128,512]{1,0:T(8,128)(2,1)}) custom-call(bf16[2,16,48,128]{3,2,1,0:T(8,128)(2,1)S(1)} %get-tuple-element.11.back, f32[128,512]{1,0:T(8,128)S(1)} %get-tuple-element.12.q_ref, ...), custom_call_target="tpu_custom_call" | custom-call | tf_op jit(solution)/shard_map/gate/pallas_call | solution.py:332

commit v5 on v4

--- a/solution.py
+++ b/solution.py
@@ -31,9 +31,26 @@
     return stacked.astype(ml_dtypes.bfloat16)
 
 
+def gated_group(back, half, g, q_ref, k_ref, v_ref, o_ref, gain_ref):
+    part = back.shape[2] // 3
+    wide = q_ref.shape[1] // HALVES
+    bf16, f32 = jnp.bfloat16, jnp.float32
+    turned = []
+    for a in range(3):
+        pieces = [back[half, g * (128 // part) + i, a * part : (a + 1) * part, :] for i in range(128 // part)]
+        turned.append(jnp.concatenate(pieces, axis=0).astype(f32).T)
+    lanes = pl.ds(pl.multiple_of(half * wide + g * 128, 128), 128)
+    q, k, v, o = q_ref[:, lanes], k_ref[:, lanes], v_ref[:, lanes], o_ref[:, lanes]
+    gain = gain_ref[:, lanes]
+    conv_out = turned[0] + gain * (k * v).astype(bf16).astype(f32)
+    conv_grad = turned[1] + gain * (o * q).astype(bf16).astype(f32)
+    values = (q * conv_out, o * conv_out, conv_grad * v, conv_grad * k, turned[2])
+    return [value.astype(bf16) for value in values]
+
+
 def exchange_kernel(
     n, q_hbm, k_hbm, v_hbm, o_hbm, taps_hbm, gain_hbm, order_hbm, tables_hbm,
-    back, q_ref, k_ref, v_ref, o_ref, gain_ref,
+    back, first_half, q_ref, k_ref, v_ref, o_ref, gain_ref,
     taps_ref, order_ref, tables, send_in, recv_tm, recv_g, recv_m2, recv_g2, recv_t2, send_out,
     mixed_s, gated_s, resp_s, sum_s, sum_f,
     load_sem, send_sem, recv_sem, pass_sem, back_send, back_recv,
@@ -42,6 +59,7 @@
     rows, channels = q_ref.shape
     own = channels // n
     part = own // HALVES
+    wide = channels // HALVES
     scale = 1.0 / math.sqrt(rows * n)
     bf16, f32 = jnp.bfloat16, jnp.float32
 
@@ -71,7 +89,7 @@
                 block = o_ref[:, cols] * q_ref[:, cols]
             turned = block.T.astype(bf16)
             for i in range(128 // part):
-                peer, half = (g * 128 + i * part) // own, i % HALVES
+                half, peer = divmod(g * (128 // part) + i, n)
                 send_in[half, peer, a * part : (a + 1) * part, :] = turned[i * part : (i + 1) * part]
 
     hops = [(h, z) for h in (1, 0) for z in (4, 3, 5, 2, 6, 1, 7, 0) if (h, z) != (0, 0)]
@@ -209,24 +227,24 @@
             values = values * factor
         send_out[half, :, a * part : (a + 1) * part, :] = values.astype(bf16).reshape(n, part, rows)
 
-    def send_result(half, start, size):
+    def send_result(half, start, size, recv):
         rws = pl.ds(start, size)
-        send_all(lambda peer: send_out.at[half, peer, rws], back.at[half, me, rws], back_send, back_recv)
+        send_all(lambda peer: send_out.at[half, peer, rws], back.at[half, me, rws], back_send, recv)
         back[half, me, rws, :] = send_out[half, me, rws, :]
 
-    def convolve(half, mixed_in, mixed_start, taps_in):
+    def convolve(half, mixed_in, mixed_start, taps_in, recv):
         response(taps_in)
         mixed_s[...] = spectra(mixed_in, mixed_start, holder).reshape(n, part, 2 * rows)
         tiles(forward_tile)
         result(half, 0, sum_s, out_tab, order)
-        send_result(half, 0, part)
-
-    def correlate(half, gated_in, start=0):
+        send_result(half, 0, part, recv)
+
+    def correlate(half, gated_in, start, recv):
         gated_s[...] = spectra(gated_in, start, holder).reshape(n, part, 2 * rows)
         tiles(backward_tile)
         result(half, 1, sum_s, out_tab, order)
         result(half, 2, sum_f, lag_tab, plain, scale)
-        send_result(half, part, 2 * part)
+        send_result(half, part, 2 * part, recv)
 
     wait_input(0)
     pass_on = pltpu.make_async_remote_copy(
@@ -235,16 +253,22 @@
         device_id={"dp": 1 - core}, device_id_type=MESH,
     )
     pass_on.start()
-    convolve(early, recv_tm, part, recv_tm)
+    convolve(early, recv_tm, part, recv_tm, back_recv.at[0])
     wait_input(1)
-    correlate(early, recv_g)
+    correlate(early, recv_g, 0, back_recv.at[0])
     pass_on.wait()
     wait_input(2)
-    convolve(late, recv_m2, 0, recv_t2)
-    correlate(late, recv_m2, part)
-
-    landed = back.at[:, pl.ds(0, n - 1)]
-    pltpu.make_async_copy(landed, landed, back_recv).wait()
+    convolve(late, recv_m2, 0, recv_t2, back_recv.at[1])
+    correlate(late, recv_m2, part, back_recv.at[1])
+
+    landed = back.at[early, pl.ds(0, n - 1)]
+    pltpu.make_async_copy(landed, landed, back_recv.at[0]).wait()
+    for g in range(wide // 128):
+        lanes = slice(g * 128, (g + 1) * 128)
+        for i, value in enumerate(gated_group(back, early, g, q_ref, k_ref, v_ref, o_ref, gain_ref)):
+            first_half[i, :, lanes] = value
+    landed = back.at[late, pl.ds(0, n - 1)]
+    pltpu.make_async_copy(landed, landed, back_recv.at[1]).wait()
     for _, _, _, recv in inputs:
         sent = recv.at[pl.ds(0, n - 1)]
         pltpu.make_async_copy(sent, sent, send_sem).wait()
@@ -253,35 +277,29 @@
 
 
 def gate_kernel(
-    n, back, q_ref, k_ref, v_ref, o_ref, gain_ref, hyena_hbm, gq_hbm, gk_hbm, gv_hbm, gf_hbm, results, sems
+    back, first_half, q_ref, k_ref, v_ref, o_ref, gain_ref,
+    hyena_hbm, gq_hbm, gk_hbm, gv_hbm, gf_hbm, second_half, sems,
 ):
     rows, channels = q_ref.shape
-    own = channels // n
-    part = own // HALVES
-    bf16, f32 = jnp.bfloat16, jnp.float32
+    wide = channels // HALVES
+    early = lax.axis_index("dp")
+    late = 1 - early
     outs = (hyena_hbm, gq_hbm, gk_hbm, gv_hbm, gf_hbm)
     stores = []
-    for g in range(channels // 128):
-        cols = slice(g * 128, (g + 1) * 128)
-        turned = []
-        for a in range(3):
-            pieces = []
-            for i in range(128 // part):
-                peer, half = (g * 128 + i * part) // own, i % HALVES
-                pieces.append(back[half, peer, a * part : (a + 1) * part, :])
-            turned.append(jnp.concatenate(pieces, axis=0).astype(f32).T)
-        q, k, v, o = q_ref[:, cols], k_ref[:, cols], v_ref[:, cols], o_ref[:, cols]
-        gain = gain_ref[:, cols]
-        conv_out = turned[0] + gain * (k * v).astype(bf16).astype(f32)
-        conv_grad = turned[1] + gain * (o * q).astype(bf16).astype(f32)
-        values = (q * conv_out, o * conv_out, conv_grad * v, conv_grad * k, turned[2])
-        for i, value in enumerate(values):
-            results[i, :, cols] = value.astype(bf16)
-            store = pltpu.make_async_copy(results.at[i, :, cols], outs[i].at[:, cols], sems.at[i, g])
-            store.start()
-            stores.append(store)
-    for store in stores:
-        store.wait()
+
+    def store(source, i, start, size, sem):
+        stores.append(pltpu.make_async_copy(source, outs[i].at[:, pl.ds(pl.multiple_of(start, 128), size)], sem))
+        stores[-1].start()
+
+    for i in range(5):
+        store(first_half.at[i], i, early * wide, wide, sems.at[0, i])
+    for g in range(wide // 128):
+        lanes = slice(g * 128, (g + 1) * 128)
+        for i, value in enumerate(gated_group(back, late, g, q_ref, k_ref, v_ref, o_ref, gain_ref)):
+            second_half[i, :, lanes] = value
+            store(second_half.at[i, :, lanes], i, late * wide + g * 128, 128, sems.at[1 + g, i])
+    for each in stores:
+        each.wait()
 
 
 def on_device(query_proj, key_proj, value_proj, filter_taps, skip_gain, out_grad, block_order):
@@ -298,9 +316,14 @@
     tables = spectrum_tables(rows)
     kept = pl.pallas_call(
         functools.partial(exchange_kernel, n),
-        out_shape=[jax.ShapeDtypeStruct(message, bf16)] + [block] * 4 + [jax.ShapeDtypeStruct((1, channels), f32)],
+        out_shape=[
+            jax.ShapeDtypeStruct(message, bf16),
+            jax.ShapeDtypeStruct((5, rows, channels // HALVES), bf16),
+            block, block, block, block,
+            jax.ShapeDtypeStruct((1, channels), f32),
+        ],
         in_specs=[hbm] * 8,
-        out_specs=[vmem] * 6,
+        out_specs=[vmem] * 7,
         scratch_shapes=[
             pltpu.VMEM((rows, channels), f32),
             pltpu.SMEM((n,), jnp.int32),
@@ -315,7 +338,7 @@
             pltpu.SemaphoreType.DMA((4,)),
             pltpu.SemaphoreType.DMA((2,)),
             pltpu.SemaphoreType.DMA(()),
-            pltpu.SemaphoreType.DMA(()),
+            pltpu.SemaphoreType.DMA((HALVES,)),
         ],
         compiler_params=pltpu.CompilerParams(
             collective_id=0, has_side_effects=True, vmem_limit_bytes=32 * 2**20
@@ -330,13 +353,13 @@
     ])
     result = jax.ShapeDtypeStruct((rows, channels), bf16)
     return pl.pallas_call(
-        functools.partial(gate_kernel, n),
+        gate_kernel,
         out_shape=[result] * 5,
-        in_specs=[vmem] * 6,
+        in_specs=[vmem] * 7,
         out_specs=[hbm] * 5,
         scratch_shapes=[
-            pltpu.VMEM((5, rows, channels), bf16),
-            pltpu.SemaphoreType.DMA((5, channels // 128)),
+            pltpu.VMEM((5, rows, channels // HALVES), bf16),
+            pltpu.SemaphoreType.DMA((1 + channels // HALVES // 128, 5)),
         ],
         compiler_params=pltpu.CompilerParams(vmem_limit_bytes=32 * 2**20),
         name="gate",

time: 29.9 us -> 29.8 us (level)
  no operation moved by 1% of the time
where the time goes in v5:
time: 29.8 us; the launch traced here: 29.7 us
  Pallas kernels  29 us (97%)
  between operations  0.64 us (2%)
    pallas_call x1, Pallas kernels, on_device(): pl.pallas_call(functools.partial(exchange_kernel, n), out_shape=[jax.Shap...  28.1 us
    pallas_call x1, Pallas kernels, on_device(): pl.pallas_call(gate_kernel, out_shape=[result] * 5, in_specs=[vmem] * 7,...  0.98 us

profile of v5, /device:TPU:8, one launch (start us, length us, event | category | flops | bytes accessed | tf_op | source)
XLA Modules:
  0.0 29.7 jit_solution(12629939582527798662)
XLA Ops:
  0.6 28.1 %exchange.1 = (bf16[2,16,48,128]{3,2,1,0:T(8,128)(2,1)S(1)}, bf16[5,128,256]{2,1,0:T(8,128)(2,1)S(1)}, f32[128,512]{1,0:T(8,128)S(1)}, f32[128,512]{1,0:T(8,128)...) custom-call(f32[128,512]{1,0:T(8,128)} %q_hbm.1, f32[128,512]{1,0:T(8,128)} %k_hbm.1, ...), custom_call_target="tpu_custom_call" | custom-call | tf_op jit(solution)/shard_map/exchange/pallas_call | solution.py:317
  28.7 1.0 %gate.1 = (bf16[128,512]{1,0:T(8,128)(2,1)}, bf16[128,512]{1,0:T(8,128)(2,1)}, bf16[128,512]{1,0:T(8,128)(2,1)}, bf16[128,512]{1,0:T(8,128)(2,1)}, bf16[128,512]{1,0:T(8,128)(2,1)}) custom-call(bf16[2,16,48,128]{3,2,1,0:T(8,128)(2,1)S(1)} %get-tuple-element.12.back, bf16[5,128,256]{2,1,0:T(8,128)(2,1)S(1)} %get-tuple-element.13.first_half, ...), custom_call_target="tpu_custom_call" | custom-call | tf_op jit(solution)/shard_map/gate/pallas_call | solution.py:355

commit v6 on v5

--- a/solution.py
+++ b/solution.py
@@ -63,9 +63,16 @@
     scale = 1.0 / math.sqrt(rows * n)
     bf16, f32 = jnp.bfloat16, jnp.float32
 
+    hops = [(h, z) for h in (1, 0) for z in (4, 3, 5, 2, 6, 1, 7, 0) if (h, z) != (0, 0)]
+    ring = n // 2
+    odd = lax.rem(me // ring, 2)
+    peers = {
+        (h, z): lax.rem(me // ring + h, 2) * ring + lax.rem(me + z + (ring - 2 * z) * odd, ring) for h, z in hops
+    }
+
     barrier = pltpu.get_barrier_semaphore()
-    for step in range(1, n):
-        pl.semaphore_signal(barrier, inc=1, device_id={"seq": lax.rem(me + step, n)}, device_id_type=MESH)
+    for hop in sorted(hops, key=lambda hop: -2 * hop[0] - min(hop[1], ring - hop[1])):
+        pl.semaphore_signal(barrier, inc=1, device_id={"seq": peers[hop]}, device_id_type=MESH)
     pl.semaphore_signal(barrier, inc=1, device_id={"dp": 1 - core}, device_id_type=MESH)
 
     loads = [
@@ -92,12 +99,6 @@
                 half, peer = divmod(g * (128 // part) + i, n)
                 send_in[half, peer, a * part : (a + 1) * part, :] = turned[i * part : (i + 1) * part]
 
-    hops = [(h, z) for h in (1, 0) for z in (4, 3, 5, 2, 6, 1, 7, 0) if (h, z) != (0, 0)]
-
-    ring = n // 2
-    peers = {
-        (h, z): lax.rem(me // ring + h, 2) * ring + lax.rem(me + z, ring) for h, z in hops
-    }
 
     def send_all(source, target, send, recv, group=None):
         for hop in group or hops:

time: 29.8 us -> 29.8 us (level)
  no operation moved by 1% of the time
where the time goes in v6:
time: 29.8 us; the launch traced here: 29.7 us
  Pallas kernels  29 us (97%)
  between operations  0.64 us (2%)
    pallas_call x1, Pallas kernels, on_device(): pl.pallas_call(functools.partial(exchange_kernel, n), out_shape=[jax.Shap...  28 us
    pallas_call x1, Pallas kernels, on_device(): pl.pallas_call(gate_kernel, out_shape=[result] * 5, in_specs=[vmem] * 7,...  0.98 us

profile of v6, /device:TPU:8, one launch (start us, length us, event | category | flops | bytes accessed | tf_op | source)
XLA Modules:
  0.0 29.7 jit_solution(8010085722152140513)
XLA Ops:
  0.6 28.0 %exchange.1 = (bf16[2,16,48,128]{3,2,1,0:T(8,128)(2,1)S(1)}, bf16[5,128,256]{2,1,0:T(8,128)(2,1)S(1)}, f32[128,512]{1,0:T(8,128)S(1)}, f32[128,512]{1,0:T(8,128)...) custom-call(f32[128,512]{1,0:T(8,128)} %q_hbm.1, f32[128,512]{1,0:T(8,128)} %k_hbm.1, ...), custom_call_target="tpu_custom_call" | custom-call | tf_op jit(solution)/shard_map/exchange/pallas_call | solution.py:318
  28.7 1.0 %gate.1 = (bf16[128,512]{1,0:T(8,128)(2,1)}, bf16[128,512]{1,0:T(8,128)(2,1)}, bf16[128,512]{1,0:T(8,128)(2,1)}, bf16[128,512]{1,0:T(8,128)(2,1)}, bf16[128,512]{1,0:T(8,128)(2,1)}) custom-call(bf16[2,16,48,128]{3,2,1,0:T(8,128)(2,1)S(1)} %get-tuple-element.12.back, bf16[5,128,256]{2,1,0:T(8,128)(2,1)S(1)} %get-tuple-element.13.first_half, ...), custom_call_target="tpu_custom_call" | custom-call | tf_op jit(solution)/shard_map/gate/pallas_call | solution.py:356

commit v7 on v6

--- a/solution.py
+++ b/solution.py
@@ -117,6 +117,8 @@
     far = [(h, z) for h, z in hops if 2 * h + min(z, 8 - z) >= 5]
     near = [hop for hop in hops if hop not in far]
 
+    partner_first = sorted(hops, key=lambda hop: hop != (1, 0))
+
     def send_input(i, group=None):
         half, start, size, recv = inputs[i]
         rws = pl.ds(start, size)
@@ -230,7 +232,7 @@
 
     def send_result(half, start, size, recv):
         rws = pl.ds(start, size)
-        send_all(lambda peer: send_out.at[half, peer, rws], back.at[half, me, rws], back_send, recv)
+        send_all(lambda peer: send_out.at[half, peer, rws], back.at[half, me, rws], back_send, recv, partner_first)
         back[half, me, rws, :] = send_out[half, me, rws, :]
 
     def convolve(half, mixed_in, mixed_start, taps_in, recv):

time: 29.8 us -> 29.8 us (level)
  no operation moved by 1% of the time
where the time goes in v7:
time: 29.8 us; the launch traced here: 29.7 us
  Pallas kernels  29 us (97%)
  between operations  0.64 us (2%)
    pallas_call x1, Pallas kernels, on_device(): pl.pallas_call(functools.partial(exchange_kernel, n), out_shape=[jax.Shap...  28 us
    pallas_call x1, Pallas kernels, on_device(): pl.pallas_call(gate_kernel, out_shape=[result] * 5, in_specs=[vmem] * 7,...  0.98 us

profile of v7, /device:TPU:8, one launch (start us, length us, event | category | flops | bytes accessed | tf_op | source)
XLA Modules:
  0.0 29.7 jit_solution(11975043451280882314)
XLA Ops:
  0.6 28.0 %exchange.1 = (bf16[2,16,48,128]{3,2,1,0:T(8,128)(2,1)S(1)}, bf16[5,128,256]{2,1,0:T(8,128)(2,1)S(1)}, f32[128,512]{1,0:T(8,128)S(1)}, f32[128,512]{1,0:T(8,128)...) custom-call(f32[128,512]{1,0:T(8,128)} %q_hbm.1, f32[128,512]{1,0:T(8,128)} %k_hbm.1, ...), custom_call_target="tpu_custom_call" | custom-call | tf_op jit(solution)/shard_map/exchange/pallas_call | solution.py:320
  28.7 1.0 %gate.1 = (bf16[128,512]{1,0:T(8,128)(2,1)}, bf16[128,512]{1,0:T(8,128)(2,1)}, bf16[128,512]{1,0:T(8,128)(2,1)}, bf16[128,512]{1,0:T(8,128)(2,1)}, bf16[128,512]{1,0:T(8,128)(2,1)}) custom-call(bf16[2,16,48,128]{3,2,1,0:T(8,128)(2,1)S(1)} %get-tuple-element.12.back, bf16[5,128,256]{2,1,0:T(8,128)(2,1)S(1)} %get-tuple-element.13.first_half, ...), custom_call_target="tpu_custom_call" | custom-call | tf_op jit(solution)/shard_map/gate/pallas_call | solution.py:358
